TPU v7x, 32 devices: a whole 2x2x4 slice. The times are simulated.
32 devices in a mesh: seq: 8 (over y, x, core), hid: 4 (over z).
Axes of the slice: x: 2, y: 2, z: 4, core: 2. Of those that a mesh axis runs over, the one named last changes fastest.
Arguments:
- patches: bfloat16 [3072, 3200], P('seq'), may hold values from -6 to 6
- norm_gain: float32 [3200], replicated, may hold values from 0.5 to 8
- query_weight: bfloat16 [3200, 2048], P(None, 'hid'), may hold values from -0.109375 to 0.109375
- key_weight: bfloat16 [3200, 2048], P(None, 'hid'), may hold values from -0.7424621 to 0.7424621
- value_weight: bfloat16 [3200, 2048], P(None, 'hid'), may hold values from -0.109375 to 0.109375
- out_weight: bfloat16 [2048, 3200], P('hid'), may hold values from -0.125 to 0.125
- layer_scale: float32 [3200], replicated, may hold values from 0.3 to 1.5
- merge_gain: float32 [12800], P('hid'), may hold values from 0.5 to 1.5
- merge_bias: float32 [12800], P('hid'), may hold values from -3 to 3
- proj_weight: bfloat16 [12800, 6144], P('hid', 'seq'), may hold values from -0.0546875 to 0.0546875
- proj_bias: float32 [6144], P('seq'), may hold values from -3 to 3
- text_rows: bfloat16 [128, 6144], P(None, 'seq'), may hold values from -6 to 6
- stream_gain: float32 [6144], P('hid'), may hold values from 0.5 to 1.5
- tile_counts: int32 [2], replicated, may hold values from 1 to 2, as said below
- image_slots: int32 [768], replicated, may hold values from 0 to 895, as said below
- text_slots: int32 [128], replicated, may hold values from 0 to 895, as said below
Outputs:
- stream: bfloat16 [896, 6144], P('seq', 'hid')
- normed: bfloat16 [896, 6144], P('seq', 'hid')
Inputs may be any that keep to these rules, and one draw needn't show every extreme that they name: `tile_counts`: the tile counts sum to 3; the largest is exactly 2. `image_slots`: image slots and text slots together name every stream position once; each image's rows lie in order at consecutive positions. `text_slots`: see image_slots; text slots increase.
All inputs are finite; a program needn't handle non-finite values.
Results may differ from a plain program's by a relative error of at most 0.022.
The roundings to bfloat16 on the way count: a program that leaves them out, or rounds other values in their place, can miss the bound.
Values may be sent and summed in bfloat16 or wider, within the bound.
A program may use at most 192 MiB of HBM per device.

v0:
```python
import jax
import jax.numpy as jnp
from jax import lax
from jax.sharding import PartitionSpec as P

HD = 128
SIDE = 32


def image_of(index_rows, tile_counts):
    bounds = jnp.cumsum(tile_counts) * (SIDE * SIDE)
    return jnp.sum((index_rows[:, None] >= bounds[None, :]).astype(jnp.int32), axis=1)


def shuffle_rows(values):
    row_count, width = values.shape
    grouped = values.reshape(row_count // (2 * SIDE), 2, SIDE // 2, 2, width)
    return grouped.transpose(0, 2, 4, 1, 3).reshape(row_count // 4, 4 * width)


def per_device(
    patches,
    norm_gain,
    query_weight,
    key_weight,
    value_weight,
    out_weight,
    layer_scale,
    merge_gain,
    merge_bias,
    proj_weight,
    proj_bias,
    text_rows,
    stream_gain,
    tile_counts,
    image_slots,
    text_slots,
):
    seq_index = lax.axis_index("seq")
    hid_index = lax.axis_index("hid")
    local_rows = patches.shape[0]
    local_heads = query_weight.shape[1] // HD
    tokens_f = patches.astype(jnp.float32)
    normed_in = (
        tokens_f * lax.rsqrt(jnp.mean(tokens_f * tokens_f, -1, keepdims=True) + 1e-06) * norm_gain
    ).astype(jnp.bfloat16)
    queries = (
        jnp.dot(normed_in, query_weight, preferred_element_type=jnp.float32) * HD ** (-0.5)
    ).astype(jnp.bfloat16)
    key_rows = jnp.dot(normed_in, key_weight, preferred_element_type=jnp.float32).astype(
        jnp.bfloat16
    )
    value_rows = jnp.dot(normed_in, value_weight, preferred_element_type=jnp.float32).astype(
        jnp.bfloat16
    )
    query_heads = queries.reshape(local_rows, local_heads, HD)
    query_ids = image_of(
        seq_index * local_rows + jnp.arange(local_rows, dtype=jnp.int32), tile_counts
    )

    def fold_block(state_now, key_block, value_block, block_start):
        maxima, totals, accumulated = state_now
        row_count = key_block.shape[0]
        key_heads = key_block.reshape(row_count, local_heads, HD)
        value_heads = value_block.reshape(row_count, local_heads, HD)
        scores = jnp.einsum(
            "qhd,khd->hqk", query_heads, key_heads, preferred_element_type=jnp.float32
        )
        key_ids = image_of(block_start + jnp.arange(row_count, dtype=jnp.int32), tile_counts)
        same_image = (query_ids[:, None] == key_ids[None, :])[None]
        scores = jnp.where(same_image, scores, jnp.float32(-1e30))
        new_max = jnp.maximum(maxima, jnp.max(scores, axis=-1))
        factor = jnp.exp(maxima - new_max)
        weights = jnp.where(same_image, jnp.exp(scores - new_max[..., None]), jnp.float32(0.0))
        totals = totals * factor + jnp.sum(weights, axis=-1)
        update = jnp.einsum(
            "hqk,khd->hqd",
            weights.astype(jnp.bfloat16),
            value_heads,
            preferred_element_type=jnp.float32,
        )
        accumulated = accumulated * factor[..., None] + update
        return (new_max, totals, accumulated)

    start_state = (
        jnp.full((local_heads, local_rows), -1e30, jnp.float32),
        jnp.zeros((local_heads, local_rows), jnp.float32),
        jnp.zeros((local_heads, local_rows, HD), jnp.float32),
    )
    key_piece = lax.all_gather(key_rows, "seq", axis=0, tiled=True)
    value_piece = lax.all_gather(value_rows, "seq", axis=0, tiled=True)
    row_count = key_piece.shape[0]
    block_rows = 512
    steps_count = row_count // block_rows
    key_blocks = key_piece.reshape(steps_count, block_rows, key_piece.shape[1])
    value_blocks = value_piece.reshape(steps_count, block_rows, value_piece.shape[1])

    def step_fn(state_in, inputs):
        key_block, value_block, index_now = inputs
        return (fold_block(state_in, key_block, value_block, index_now * block_rows), None)

    result, unused = lax.scan(
        step_fn, start_state, (key_blocks, value_blocks, jnp.arange(steps_count, dtype=jnp.int32))
    )
    maxima, totals, accumulated = result
    attended = (accumulated / totals[..., None]).astype(jnp.bfloat16)
    attended = attended.transpose(1, 0, 2).reshape(local_rows, local_heads * HD)
    branch_part = jnp.dot(attended, out_weight, preferred_element_type=jnp.float32)
    branch = lax.psum(branch_part.astype(jnp.bfloat16), "hid").astype(jnp.float32)
    merged = shuffle_rows(tokens_f + layer_scale * branch)
    mean_row = jnp.mean(merged, -1, keepdims=True)
    var_row = jnp.mean(merged * merged, -1, keepdims=True) - mean_row * mean_row
    block_width = merged.shape[1] // lax.axis_size("hid")
    merged_block = lax.dynamic_slice_in_dim(merged, hid_index * block_width, block_width, 1)
    merged_normed = (
        (merged_block - mean_row) * lax.rsqrt(var_row + 1e-05) * merge_gain + merge_bias
    ).astype(jnp.bfloat16)
    partial_proj = jnp.dot(
        lax.all_gather(merged_normed, "seq", axis=0, tiled=True),
        proj_weight,
        preferred_element_type=jnp.float32,
    )
    stream_size = image_slots.shape[0] + text_slots.shape[0]
    summed = lax.psum(partial_proj.astype(jnp.bfloat16), "hid").astype(jnp.float32)
    image_rows = jax.nn.gelu(summed + proj_bias, approximate=False).astype(jnp.bfloat16)
    stream_cols = (
        jnp.zeros((stream_size, image_rows.shape[1]), jnp.bfloat16)
        .at[image_slots]
        .set(image_rows)
        .at[text_slots]
        .set(text_rows)
    )
    stream_full = lax.all_to_all(stream_cols, "seq", split_axis=0, concat_axis=1, tiled=True)
    stream_f = stream_full.astype(jnp.float32)
    inverse_rms = lax.rsqrt(jnp.mean(stream_f * stream_f, -1, keepdims=True) + 1e-05)
    out_width = stream_full.shape[1] // lax.axis_size("hid")
    stream_share = lax.dynamic_slice_in_dim(stream_full, hid_index * out_width, out_width, 1)
    normed_share = (stream_share.astype(jnp.float32) * inverse_rms * stream_gain).astype(
        jnp.bfloat16
    )
    return (stream_share, normed_share)


def solution(mesh):
    return jax.shard_map(
        per_device,
        mesh=mesh,
        in_specs=(
            P("seq", None),
            P(),
            P(None, "hid"),
            P(None, "hid"),
            P(None, "hid"),
            P("hid", None),
            P(),
            P("hid"),
            P("hid"),
            P("hid", "seq"),
            P("seq"),
            P(None, "seq"),
            P("hid"),
            P(),
            P(),
            P(),
        ),
        out_specs=(P("seq", "hid"), P("seq", "hid")),
        check_vma=False,
    )
```

profile of v0, /device:TPU:0, one launch (start us, length us, event | category | flops | bytes accessed | tf_op | source)
XLA Modules:
  0.0 558.1 jit_solution(17785642322332899441)
XLA Ops:
  7.2 2.4 fusion.16
  9.8 4.2 convolution_convert_fusion.3
  14.1 5.0 convolution_convert_fusion.2
  19.2 4.2 fusion.33
  24.5 24.7 %all-gather.4.cloned.1.call-done = bf16[3072,512]{1,0:T(8,128)(2,1)} async-done(((bf16[384,512]{1,0:T(8,128)(2,1)}), bf16[3072,512]{1,0:T(8,128)(2,1)}) %all-gather.4.cloned.1.call-update) | async-done | bytes 3145744 | tf_op jit(solution)/shard_map/all_gather | solution.py:90
  49.3 34.2 %all-gather.6.cloned.1.call-done = bf16[3072,512]{1,0:T(8,128)(2,1)} async-done(((bf16[384,512]{1,0:T(8,128)(2,1)}), bf16[3072,512]{1,0:T(8,128)(2,1)}) %all-gather.6.cloned.1.call-update) | async-done | bytes 3145744 | tf_op jit(solution)/shard_map/all_gather | solution.py:91
  83.5 110.1 %while.17 = (s32[]{:T(128)}, f32[4,384]{1,0:T(4,128)S(1)}, f32[4,384]{1,0:T(4,128)S(1)}, f32[4,384,128]{2,1,0:T(8,128)}, s32[384]{0:T(512)S(1)}, /*index=5*/s32[...) while((s32[]{:T(128)}, f32[4,384]{1,0:T(4,128)S(1)}, ...), condition=%wide.region_7.8_spmd.clone, body=%wide.region_3.7_spmd.clone.sunk | while | flops 411314688 | bytes 17540800 | solution.py:102
  85.0 2.3 constant_dynamic-slice_fusion.6
  87.4 2.1 copy.79
  89.4 3.6 fusion.65
  93.0 2.6 fusion.66
  95.6 2.1 copy.80
  97.6 4.0 fusion.68
  103.2 2.3 constant_dynamic-slice_fusion.6
  105.5 2.1 copy.79
  107.6 3.6 fusion.65
  111.1 2.6 fusion.66
  113.7 2.1 copy.80
  115.8 4.3 fusion.68
  121.6 2.3 constant_dynamic-slice_fusion.6
  123.9 2.1 copy.79
  125.9 3.6 fusion.65
  129.5 2.6 fusion.66
  132.1 2.1 copy.80
  134.2 4.3 fusion.68
  140.0 2.3 constant_dynamic-slice_fusion.6
  142.3 2.1 copy.79
  144.3 3.6 fusion.65
  147.9 2.6 fusion.66
  150.5 2.1 copy.80
  152.6 4.3 fusion.68
  158.4 2.3 constant_dynamic-slice_fusion.6
  160.7 2.1 copy.79
  162.7 3.6 fusion.65
  166.3 2.6 fusion.66
  168.9 2.1 copy.80
  171.0 4.3 fusion.68
  176.7 2.3 constant_dynamic-slice_fusion.6
  179.1 2.1 copy.79
  181.1 3.6 fusion.65
  184.7 2.6 fusion.66
  187.3 2.1 copy.80
  189.3 4.3 fusion.68
  193.6 2.3 copy.63
  195.9 1.2 divide_convert_fusion
  197.1 3.0 convolution_convert_fusion
  200.3 98.7 %all-reduce.3.cloned.1.call-done = bf16[384,3200]{1,0:T(8,128)(2,1)} async-done(((bf16[384,3200]{1,0:T(8,128)(2,1)}), bf16[384,3200]{1,0:T(8,128)(2,1)}) %all-reduce.3.cloned.1.call-update) | async-done | bytes 2457616 | tf_op jit(solution)/shard_map/psum | solution.py:109
  299.1 4.5 convert_add_fusion
  303.6 6.8 %reshape.161 = f32[6,2,16,2,3200]{4,3,2,1,0:T(2,128)} reshape(f32[384,3200]{1,0:T(8,128)} %convert_add_fusion) | data formatting | bytes 9830400 | tf_op jit(solution)/shard_map/reshape | solution.py:17
  310.3 39.8 %copy.64 = f32[6,2,16,2,3200]{2,0,3,1,4:T(8,128)} copy(f32[6,2,16,2,3200]{4,3,2,1,0:T(2,128)} %reshape.161) | data formatting | bytes 9830400 | tf_op jit(solution)/shard_map/reshape | solution.py:17
  350.1 17.3 %bitcast_reduce_fusion = (f32[6,16]{1,0:T(8,128)S(1)}, f32[6,16]{1,0:T(8,128)S(1)}) fusion(f32[6,2,16,2,3200]{2,0,3,1,4:T(8,128)} %copy.64), kind=kLoop, calls=%fused_computation.83 | loop fusion | flops 3686208 | bytes 4915968 | tf_op jit(solution)/shard_map/reduce_sum | solution.py:111
  367.5 31.2 %reshape.162 = f32[96,12800]{0,1:T(8,128)} reshape(f32[6,16,3200,2,2]{1,0,4,3,2:T(8,128)} %bitcast.71) | data formatting | bytes 9830400 | tf_op jit(solution)/shard_map/reshape | solution.py:18
  398.7 1.6 constant_dynamic-slice_fusion.3
  400.8 1.1 add_convert_fusion
  402.0 38.8 %all-gather.8.cloned.1.call-done = bf16[768,3200]{1,0:T(8,128)(2,1)} async-done(((bf16[96,3200]{1,0:T(8,128)(2,1)}), bf16[768,3200]{1,0:T(8,128)(2,1)}) %all-gather.8.cloned.1.call-update) | async-done | bytes 4915216 | tf_op jit(solution)/shard_map/all_gather | solution.py:119
  440.8 9.0 %convolution_convert_fusion.1 = bf16[768,768]{1,0:T(8,128)(2,1)} fusion(bf16[768,3200]{1,0:T(8,128)(2,1)} %all-gather.8.cloned.1.call-done, bf16[3200,768]{1,0:T(8,128)(2,1)} %param.27), kind=kOutput, calls=%fused_computation.58 | convolution fusion | flops 3775463424 | bytes 11010048 | tf_op jit(solution)/shard_map/dot_general | solution.py:118
  449.9 56.0 %all-reduce.5.cloned.1.call-done = bf16[768,768]{1,0:T(8,128)(2,1)} async-done(((bf16[768,768]{1,0:T(8,128)(2,1)}), bf16[768,768]{1,0:T(8,128)(2,1)}) %all-reduce.5.cloned.1.call-update) | async-done | bytes 1179664 | tf_op jit(solution)/shard_map/psum | solution.py:124
  506.0 14.4 %scatter_custom_fusion = bf16[896,768]{1,0:T(8,128)(2,1)} fusion(s32[768]{0:T(1024)S(1)} %compare_select_fusion, bf16[]{:T(256)} %constant.65.clone.1, bf16[768,768]{1,0:T(8,128)(2,1)} %all-reduce.5.cloned.1.call-done, f32[]{:T(128)} %constant.134.clone.1, f32[]{:T(128)} %constant.133.clone.1, f32[]{:T(128)} %constant.132.clone.1, f32[]{:T(128)} %constant.42.clone.1, ...), kind=kCustom, calls=%fused_computation.67 | custom fusion | flops 39518208 | bytes 2560058 | tf_op jit(solution)/shard_map/scatter | solution.py:129
  520.4 3.7 scatter_fusion
  524.1 4.3 all-to-all-start
  528.4 18.9 %all-to-all-done = bf16[8,112,768]{2,1,0:T(8,128)(2,1)} async-done(((bf16[8,112,768]{2,1,0:T(8,128)(2,1)}), bf16[8,112,768]{2,1,0:T(8,128)(2,1)}, u32[]{:S(2)}, u32[]{:S(2)}) %all-to-all-start) | async-done | bytes 1376288 | tf_op jit(solution)/shard_map/all_to_all | solution.py:133
  547.3 1.6 copy.74
  548.9 1.7 multiply_reduce_fusion.1
  550.7 0.9 multiply_convert_fusion
  (104 shorter events, 7.7 us)
Async XLA Ops:
  7.2 189.9 %copy-start = (bf16[512,3200]{1,0:T(8,128)(2,1)S(1)}, bf16[512,3200]{1,0:T(8,128)(2,1)}, u32[]{:S(2)}) copy-start(bf16[512,3200]{1,0:T(8,128)(2,1)} %param.23) | copy-start | bytes 9830404
  7.2 42.1 %all-gather.4.cloned.1.call-start = ((), (), s32[]{:S(2)}) async-start(), calls=%async_computation.1 | async-start | bytes 3538944 | tf_op jit(solution)/shard_map/all_gather | solution.py:90
  7.2 2.6 copy-start.2
  9.8 4.3 copy-start.11
  14.1 69.4 %all-gather.6.cloned.1.call-start = ((), (), s32[]{:S(2)}) async-start(), calls=%async_computation.2 | async-start | bytes 3538944 | tf_op jit(solution)/shard_map/all_gather | solution.py:91
  19.2 279.9 %all-reduce.3.cloned.1.call-start = ((), (), s32[]{:S(2)}) async-start(), calls=%async_computation.3 | async-start | bytes 4915200 | tf_op jit(solution)/shard_map/psum | solution.py:109
  19.2 5.0 copy-start.12
  197.1 102.0 %copy-start.5 = (f32[3200]{0:T(1024)S(1)}, f32[3200]{0:T(1024)}, u32[]{:S(2)}) copy-start(f32[3200]{0:T(1024)} %param.24) | copy-start | bytes 38404
  200.1 99.0 %copy-start.3 = (bf16[384,3200]{1,0:T(8,128)(2,1)S(1)}, bf16[384,3200]{1,0:T(8,128)(2,1)}, u32[]{:S(2)}) copy-start(bf16[384,3200]{1,0:T(8,128)(2,1)} %param.18) | copy-start | bytes 7372804
  200.1 240.7 %all-gather.8.cloned.1.call-start = ((), (), s32[]{:S(2)}) async-start(), calls=%async_computation.4 | async-start | bytes 5529600 | tf_op jit(solution)/shard_map/all_gather | solution.py:119
  398.7 2.1 copy-start.6
  398.7 2.1 copy-start.7
  401.9 48.0 %copy-start.13 = (s32[128]{0:T(128)S(1)}, s32[128]{0:T(128)}, u32[]{:S(2)}) copy-start(s32[128]{0:T(128)} %param.33) | copy-start | bytes 1540
  401.9 48.0 %copy-start.10 = (s32[768]{0:T(1024)S(1)}, s32[768]{0:T(1024)}, u32[]{:S(2)}) copy-start(s32[768]{0:T(1024)} %param.32) | copy-start | bytes 9220
  401.9 104.0 %copy-start.9 = (f32[768]{0:T(1024)S(1)}, f32[768]{0:T(1024)}, u32[]{:S(2)}) copy-start(f32[768]{0:T(1024)} %param.28) | copy-start | bytes 9220
  401.9 104.0 %all-reduce.5.cloned.1.call-start = ((), (), s32[]{:S(2)}) async-start(), calls=%async_computation.5 | async-start | bytes 2359296 | tf_op jit(solution)/shard_map/psum | solution.py:124
  449.9 70.5 %copy-start.4 = (bf16[128,768]{1,0:T(8,128)(2,1)S(1)}, bf16[128,768]{1,0:T(8,128)(2,1)}, u32[]{:S(2)}) copy-start(bf16[128,768]{1,0:T(8,128)(2,1)} %param.29) | copy-start | bytes 589828
  524.1 23.2 %all-to-all-start = ((bf16[8,112,768]{2,1,0:T(8,128)(2,1)}), bf16[8,112,768]{2,1,0:T(8,128)(2,1)}, u32[]{:S(2)}, u32[]{:S(2)}) async-start(bf16[8,112,768]{2,1,0:T(8,128)(2,1)} %bitcast.7), calls=%async_computation | async-start | bytes 2752512 | tf_op jit(solution)/shard_map/all_to_all | solution.py:133
  528.4 22.3 %copy-start.8 = (f32[1536]{0:T(1024)S(1)}, f32[1536]{0:T(1024)}, u32[]{:S(2)}) copy-start(f32[1536]{0:T(1024)} %param.30) | copy-start | bytes 18436
  547.3 4.3 copy-start.1
Sparse Core Ops, SparseCore 0:
  14.2 35.0 all-gather.3
  51.1 32.3 all-gather.5
  200.2 98.7 all-reduce.2
  402.0 38.7 all-gather.7
  450.0 55.8 all-reduce.4
where the time goes:
time: 560 us; the launch traced here: 558 us
  waiting for transfers between devices  272 us (49%)
  local copies, waits for them, and re-layouts  131 us (23%)
  matrix products  72.2 us (13%)
  other arithmetic  61 us (11%)
  between operations  14 us (2%)
    psum x1, waiting for transfers between devices, per_device(): lax.psum(branch_part.astype(jnp.bfloat16), 'hid').astype(jnp.float32)  98.7 us
    psum x1, waiting for transfers between devices, per_device(): lax.psum(partial_proj.astype(jnp.bfloat16), 'hid').astype(jnp.float32)  56 us
    reshape x2, local copies, waits for them, and re-layouts, shuffle_rows(): grouped = values.reshape(row_count // (2 * SIDE), 2, SIDE // 2, 2, width)  46.5 us
    dynamic_slice x24, local copies, waits for them, and re-layouts, per_device(): lax.scan(step_fn, start_state, (key_blocks, value_blocks, jnp.arange(step...  42.1 us
    all_gather x1, waiting for transfers between devices, per_device(): lax.all_gather(merged_normed, 'seq', axis=0, tiled=True)  38.8 us
    all_gather x1, waiting for transfers between devices, per_device(): value_piece = lax.all_gather(value_rows, 'seq', axis=0, tiled=True)  34.2 us
    reshape x1, local copies, waits for them, and re-layouts, shuffle_rows(): return grouped.transpose(0, 2, 4, 1, 3).reshape(row_count // 4, 4 * width)  31.2 us
    dot_general x6, matrix products, fold_block(): jnp.einsum('hqk,khd->hqd', weights.astype(jnp.bfloat16), value_heads, pre...  25.4 us
  transfers between devices with their start and end apart: 6, of which 6 were waited for; matrix products, arithmetic and copies ran while one was open for 2% of the time, Pallas kernels for 0%

commit v1 on v0

v1 whole, which is shorter than its diff:
```python
import functools

import jax
import jax.numpy as jnp
from jax import lax
from jax.experimental import pallas as pl
from jax.experimental.pallas import tpu as pltpu
from jax.sharding import PartitionSpec as P

HD = 128
SIDE = 32
TILE = SIDE * SIDE
BLOCK = 128
MESH = pl.DeviceIdType.MESH
F32 = jnp.float32
BF16 = jnp.bfloat16
VMEM = pl.BlockSpec(memory_space=pltpu.VMEM)
LIMIT = 50 * 1024 * 1024


def params(number):
    return pltpu.CompilerParams(
        collective_id=number, has_side_effects=True, vmem_limit_bytes=LIMIT
    )


def greet(peers):
    barrier = pltpu.get_barrier_semaphore()
    for peer in peers:
        pl.semaphore_signal(barrier, inc=1, device_id=peer, device_id_type=MESH)
    pl.semaphore_wait(barrier, len(peers))


def remote(src, dst, send_sem, recv_sem, peer):
    return pltpu.make_async_remote_copy(
        src_ref=src,
        dst_ref=dst,
        send_sem=send_sem,
        recv_sem=recv_sem,
        device_id=peer,
        device_id_type=MESH,
    )


def head_cols(index):
    return pl.ds(pl.multiple_of(index * HD, HD), HD)


def exchange_kernel(L, G, q_ref, k_ref, v_ref, qo, ko, vo, send1, recv1, send2, recv2):
    s = lax.axis_index("seq")
    c, k = s // G, s % G
    places = [(c + t) % L for t in range(1, L)]
    mates = [(k + t) % G for t in range(1, G)]
    greet([{"seq": o * G + k} for o in places] + [{"seq": c * G + m} for m in mates])
    ins, outs = (k_ref, v_ref, q_ref), (ko, vo, qo)
    sent = []
    for t, o in enumerate(places):
        for a in range(3):
            copy = remote(
                ins[a].at[:, head_cols(o)], outs[a].at[s], send1.at[t, a], recv1.at[c, a],
                {"seq": o * G + k},
            )
            copy.start()
            sent.append(copy)
    own = head_cols(c)
    for a in range(3):
        outs[a][s] = ins[a][:, own]

    def share(t, slot, home):
        for u, m in enumerate(mates):
            for a in range(2):
                copy = remote(
                    outs[a].at[slot], outs[a].at[slot], send2.at[t, u, a], recv2.at[home, k, a],
                    {"seq": c * G + m},
                )
                copy.start()
                sent.append(copy)

    share(0, s, c)
    for t in range(1, L):
        o = (c - t + L) % L
        for a in range(3):
            remote(
                outs[a].at[o * G + k], outs[a].at[o * G + k], send1.at[0, a], recv1.at[o, a],
                {"seq": o * G + k},
            ).wait_recv()
        share(t, o * G + k, o)
    for m in mates:
        for t in range(L):
            o = (c + t) % L
            for a in range(2):
                remote(
                    outs[a].at[o * G + m], outs[a].at[o * G + m], send2.at[0, 0, a],
                    recv2.at[o, m, a], {"seq": c * G + m},
                ).wait_recv()
    for copy in sent:
        copy.wait_send()


def exchange(q, k, v, S, L):
    G = S // L
    rows = q.shape[0]
    shape = jax.ShapeDtypeStruct((S, rows, HD), BF16)
    return pl.pallas_call(
        functools.partial(exchange_kernel, L, G),
        out_shape=(shape,) * 3,
        in_specs=[VMEM] * 3,
        out_specs=(VMEM,) * 3,
        scratch_shapes=[
            pltpu.SemaphoreType.DMA((L, 3)),
            pltpu.SemaphoreType.DMA((L, 3)),
            pltpu.SemaphoreType.DMA((L, G, 2)),
            pltpu.SemaphoreType.DMA((L, G, 2)),
        ],
        compiler_params=params(0),
        name="exchange_heads",
    )(q, k, v)


def attend_kernel(G, rows, lo, hi, place, q_ref, k_ref, v_ref, out_ref):
    first = (pl.program_id(0) * G + place[0]) * rows + pl.program_id(1) * BLOCK
    tile = lax.div(first, TILE)
    q = q_ref[0]

    def step(t, carry):
        top, total, acc = carry
        span = pl.ds(pl.multiple_of(t * TILE, TILE), TILE)
        scores = lax.dot_general(
            q, k_ref[span, :], (((1,), (1,)), ((), ())), preferred_element_type=F32
        )
        new_top = jnp.maximum(top, jnp.max(scores, axis=1, keepdims=True))
        factor = jnp.exp(top - new_top)
        weights = jnp.exp(scores - new_top)
        total = total * factor + jnp.sum(weights, axis=1, keepdims=True)
        acc = acc * factor + jnp.dot(
            weights.astype(BF16), v_ref[span, :], preferred_element_type=F32
        )
        return new_top, total, acc

    start = (
        jnp.full((BLOCK, 1), -1e30, F32),
        jnp.zeros((BLOCK, 1), F32),
        jnp.zeros((BLOCK, HD), F32),
    )
    top, total, acc = lax.fori_loop(lo[tile], hi[tile], step, start)
    out_ref[0] = (acc / total).astype(BF16)


def attend(q, k, v, lo, hi, place, S, L):
    G = S // L
    rows = q.shape[1]
    return pl.pallas_call(
        functools.partial(attend_kernel, G, rows),
        out_shape=jax.ShapeDtypeStruct((L, rows, HD), BF16),
        grid_spec=pltpu.PrefetchScalarGridSpec(
            num_scalar_prefetch=3,
            grid=(L, rows // BLOCK),
            in_specs=[
                pl.BlockSpec((1, BLOCK, HD), lambda a, b, lo, hi, p: (a * G + p[0], b, 0)),
                VMEM,
                VMEM,
            ],
            out_specs=pl.BlockSpec((1, BLOCK, HD), lambda a, b, lo, hi, p: (a, b, 0)),
        ),
        compiler_params=pltpu.CompilerParams(vmem_limit_bytes=LIMIT),
        name="attend",
    )(lo, hi, place, q, k.reshape(S * rows, HD), v.reshape(S * rows, HD))


def spread_kernel(L, G, H, a_ref, out, send, recv):
    s, h = lax.axis_index("seq"), lax.axis_index("hid")
    c, k = s // G, s % G
    peers = [
        ((c + dc) % L, (h + dh) % H) for dh in range(H) for dc in range(L) if dc or dh
    ]
    ids = [{"seq": o * G + k, "hid": z} for o, z in peers]
    greet(ids)
    mine = h * L + c
    sent = []
    for t, (o, z) in enumerate(peers):
        copy = remote(
            a_ref.at[o], out.at[:, head_cols(mine)], send.at[t], recv.at[mine], ids[t]
        )
        copy.start()
        sent.append(copy)
    out[:, head_cols(mine)] = a_ref[c]
    for t, (o, z) in enumerate(peers):
        source = z * L + o
        remote(
            a_ref.at[o], out.at[:, head_cols(source)], send.at[t], recv.at[source], ids[t]
        ).wait_recv()
    for copy in sent:
        copy.wait_send()


def spread(a, S, L, H):
    rows = a.shape[1]
    return pl.pallas_call(
        functools.partial(spread_kernel, L, S // L, H),
        out_shape=jax.ShapeDtypeStruct((rows, H * L * HD), BF16),
        in_specs=[VMEM],
        out_specs=VMEM,
        scratch_shapes=[
            pltpu.SemaphoreType.DMA((H * L,)),
            pltpu.SemaphoreType.DMA((H * L,)),
        ],
        compiler_params=params(1),
        name="spread_attended",
    )(a)


def merge_kernel(
    L, G, H, a_ref, w_ref, x_ref, ls_ref, gain_ref, bias_ref, out,
    res, stats, lanes, place, ssend, srecv, send1, recv1, send2, recv2,
):
    s, h = lax.axis_index("seq"), lax.axis_index("hid")
    c, k = s // G, s % G
    planes = [(h + t) % H for t in range(1, H)]
    places = [(c + t) % L for t in range(1, L)]
    mates = [(k + t) % G for t in range(1, G)]
    greet(
        [{"hid": z} for z in planes]
        + [{"seq": o * G + k} for o in places]
        + [{"seq": c * G + m} for m in mates]
    )
    rows, width = x_ref.shape
    sub = BLOCK // 4
    full = width // HD
    for b in range(rows // BLOCK):
        span = slice(b * BLOCK, (b + 1) * BLOCK)
        branch = jnp.dot(a_ref[span, :], w_ref[...], preferred_element_type=F32)
        value = x_ref[span, :].astype(F32) + ls_ref[...] * branch
        res[span, :] = value
        one = jnp.sum(value, axis=1, keepdims=True)
        two = jnp.sum(value * value, axis=1, keepdims=True)
        for n, column in ((0, one), (1, two)):
            summed = sum(column[q * sub : (q + 1) * sub] for q in range(4))
            stats[h, n, b * sub : (b + 1) * sub, :] = jnp.broadcast_to(summed, (sub, HD))
    sent = []
    for t, z in enumerate(planes):
        copy = remote(stats.at[h], stats.at[h], ssend.at[t], srecv.at[h], {"hid": z})
        copy.start()
        sent.append(copy)
    lanes[...] = jnp.zeros_like(lanes)
    row = lax.broadcasted_iota(jnp.int32, (4 * HD, 4 * HD), 0)
    col = lax.broadcasted_iota(jnp.int32, (4 * HD, 4 * HD), 1)
    place[...] = jnp.where(col == 4 * (row % HD) + lax.div(row, HD), 1.0, 0.0).astype(BF16)
    for t, z in enumerate(planes):
        remote(stats.at[z], stats.at[z], ssend.at[t], srecv.at[z], {"hid": z}).wait_recv()
    total = stats[0]
    for z in range(1, H):
        total = total + stats[z]
    total = total * (1.0 / (4 * width * H))
    mean = total[0]
    scale = lax.rsqrt(total[1] - mean * mean + 1e-05)
    for b in range(rows // BLOCK):
        part = slice(b * sub, (b + 1) * sub)
        mean_b, scale_b = mean[part, :1], scale[part, :1]
        for q in range(4):
            start = b * BLOCK + q * sub
            value = (res[start : start + sub, :] - mean_b) * scale_b
            value = (value * gain_ref[q : q + 1, :] + bias_ref[q : q + 1, :]).astype(BF16)
            for j in range(full):
                lanes[part, (4 * j + q) * HD : (4 * j + q + 1) * HD] = value[:, j * HD : (j + 1) * HD]
            if width % HD:
                at = (4 * full + q) * HD
                lanes[part, at : at + width % HD] = value[:, full * HD :]
    for j in range(full):
        cols = slice(4 * j * HD, 4 * (j + 1) * HD)
        out[s, :, cols] = jnp.dot(
            lanes[:, cols], place[...], preferred_element_type=F32
        ).astype(BF16)
    if width % HD:
        cols = slice(4 * full * HD, 4 * (full + 1) * HD)
        left = 4 * (width % HD)
        last = jnp.dot(lanes[:, cols], place[...], preferred_element_type=F32)
        out[s, :, 4 * full * HD :] = last[:, :left].astype(BF16)
    for t, o in enumerate(places):
        copy = remote(out.at[s], out.at[s], send1.at[t], recv1.at[c], {"seq": o * G + k})
        copy.start()
        sent.append(copy)

    def share(t, slot, home):
        for u, m in enumerate(mates):
            copy = remote(
                out.at[slot], out.at[slot], send2.at[t, u], recv2.at[home, k], {"seq": c * G + m}
            )
            copy.start()
            sent.append(copy)

    share(0, s, c)
    for t in range(1, L):
        o = (c - t + L) % L
        slot = o * G + k
        remote(out.at[slot], out.at[slot], send1.at[0], recv1.at[o], {"seq": slot}).wait_recv()
        share(t, slot, o)
    for m in mates:
        for t in range(L):
            o = (c + t) % L
            slot = o * G + m
            remote(
                out.at[slot], out.at[slot], send2.at[0, 0], recv2.at[o, m], {"seq": c * G + m}
            ).wait_recv()
    for copy in sent:
        copy.wait_send()


def merge(a, w, x, ls, gain, bias, S, L, H):
    G = S // L
    rows, width = x.shape
    return pl.pallas_call(
        functools.partial(merge_kernel, L, G, H),
        out_shape=jax.ShapeDtypeStruct((S, rows // 4, 4 * width), BF16),
        in_specs=[VMEM] * 6,
        out_specs=VMEM,
        scratch_shapes=[
            pltpu.VMEM((rows, width), F32),
            pltpu.VMEM((H, 2, rows // 4, HD), F32),
            pltpu.VMEM((rows // 4, 4 * HD * pl.cdiv(width, HD)), BF16),
            pltpu.VMEM((4 * HD, 4 * HD), BF16),
            pltpu.SemaphoreType.DMA((H,)),
            pltpu.SemaphoreType.DMA((H,)),
            pltpu.SemaphoreType.DMA((L,)),
            pltpu.SemaphoreType.DMA((L,)),
            pltpu.SemaphoreType.DMA((L, G)),
            pltpu.SemaphoreType.DMA((L, G)),
        ],
        compiler_params=params(2),
        name="merge_rows",
    )(a, w, x, ls, gain, bias)


def finish_kernel(
    g, H, p_ref, bias_ref, text_ref, mask_ref, gain_ref, stream, normed,
    parts, rows_out, rows_in, squares, send1, recv1, send2, recv2, send3, recv3,
):
    s, h = lax.axis_index("seq"), lax.axis_index("hid")
    c, k = s // g, s % g
    planes = [(h + t) % H for t in range(1, H)]
    off = c != h
    barrier = pltpu.get_barrier_semaphore()
    for z in planes:
        pl.semaphore_signal(barrier, inc=1, device_id={"hid": z}, device_id_type=MESH)
    for t in range(g):
        j = (k + t) % g
        partner = {"seq": g * h + j, "hid": c}
        if t:
            pl.semaphore_signal(barrier, inc=1, device_id=partner, device_id_type=MESH)
        else:
            @pl.when(off)
            def _():
                pl.semaphore_signal(barrier, inc=1, device_id=partner, device_id_type=MESH)
    pl.semaphore_wait(barrier, len(planes) + g - 1 + off.astype(jnp.int32))

    sent = []
    for t, z in enumerate(planes):
        copy = remote(p_ref.at[z], parts.at[h], send1.at[t], recv1.at[h], {"hid": z})
        copy.start()
        sent.append(copy)
    for t, z in enumerate(planes):
        remote(p_ref.at[z], parts.at[z], send1.at[t], recv1.at[z], {"hid": z}).wait_recv()
    part_rows = stream.shape[0]
    width = bias_ref.shape[1]
    for j in range(g):
        span = slice(j * part_rows, (j + 1) * part_rows)
        value = p_ref[h, span, :].astype(F32)
        for z in planes:
            value = value + parts[z, span, :].astype(F32)
        value = value + bias_ref[...]
        value = value * (lax.erf(value * F32(0.7071067811865476)) + 1.0) * 0.5
        rows_out[j] = jnp.where(
            mask_ref[span, :1] > 0.5, value, text_ref[span, :].astype(F32)
        ).astype(BF16)
    for t in range(g):
        j = (k + t) % g
        partner = {"seq": g * h + j, "hid": c}
        copy = remote(rows_out.at[j], rows_in.at[k], send2.at[t], recv2.at[k], partner)
        if t:
            copy.start()
            sent.append(copy)
        else:
            pl.when(off)(copy.start)

            @pl.when(jnp.logical_not(off))
            def _():
                rows_in[k] = rows_out[k]

    for t in range(g):
        j = (k + t) % g
        partner = {"seq": g * h + j, "hid": c}
        copy = remote(rows_out.at[j], rows_in.at[j], send2.at[t], recv2.at[j], partner)
        if t:
            copy.wait_recv()
        else:
            @pl.when(off)
            def _():
                copy.wait_recv()
                copy.wait_send()
    square = jnp.zeros((part_rows, 1), F32)
    for j in range(g):
        value = rows_in[j]
        stream[:, j * width : (j + 1) * width] = value
        value = value.astype(F32)
        square = square + jnp.sum(value * value, axis=1, keepdims=True)
    squares[h] = jnp.broadcast_to(square, squares.shape[1:])
    for t, z in enumerate(planes):
        copy = remote(squares.at[h], squares.at[h], send3.at[t], recv3.at[h], {"hid": z})
        copy.start()
        sent.append(copy)
    for t, z in enumerate(planes):
        remote(squares.at[z], squares.at[z], send3.at[t], recv3.at[z], {"hid": z}).wait_recv()
    total = squares[0]
    for z in range(1, H):
        total = total + squares[z]
    scale = lax.rsqrt(total * (1.0 / (g * width * H)) + 1e-05)[:, :1]
    normed[...] = (stream[...].astype(F32) * scale * gain_ref[...]).astype(BF16)
    for copy in sent:
        copy.wait_send()


def finish(placed, bias, text, mask, gain, S, H):
    g = S // H
    width = placed.shape[-1]
    part_rows = placed.shape[1] // g
    shape = jax.ShapeDtypeStruct((part_rows, g * width), BF16)
    return pl.pallas_call(
        functools.partial(finish_kernel, g, H),
        out_shape=(shape, shape),
        in_specs=[VMEM] * 5,
        out_specs=(VMEM, VMEM),
        scratch_shapes=[
            pltpu.VMEM((H, g * part_rows, width), BF16),
            pltpu.VMEM((g, part_rows, width), BF16),
            pltpu.VMEM((g, part_rows, width), BF16),
            pltpu.VMEM((H, part_rows, HD), F32),
            pltpu.SemaphoreType.DMA((H,)),
            pltpu.SemaphoreType.DMA((H,)),
            pltpu.SemaphoreType.DMA((g,)),
            pltpu.SemaphoreType.DMA((g,)),
            pltpu.SemaphoreType.DMA((H,)),
            pltpu.SemaphoreType.DMA((H,)),
        ],
        compiler_params=params(3),
        name="finish_rows",
    )(placed, bias, text, mask, gain)


def grouping():
    new = jnp.arange(BLOCK, dtype=jnp.int32)
    half = SIDE // 2
    quarter = BLOCK // 4
    spot, rest = new // quarter, new % quarter
    pair, c2 = rest // half, rest % half
    old = (2 * pair + spot // 2) * SIDE + 2 * c2 + spot % 2
    return (old[:, None] == new[None, :]).astype(BF16)


def per_device(
    patches,
    norm_gain,
    query_weight,
    key_weight,
    value_weight,
    out_weight,
    layer_scale,
    merge_gain,
    merge_bias,
    proj_weight,
    proj_bias,
    text_rows,
    stream_gain,
    tile_counts,
    image_slots,
    text_slots,
):
    S, H = lax.axis_size("seq"), lax.axis_size("hid")
    s, h = lax.axis_index("seq"), lax.axis_index("hid")
    rows, depth = patches.shape
    L = query_weight.shape[1] // HD
    G = S // L
    quarter = depth // H

    head_rows = out_weight.shape[0]
    piece = head_rows // S
    own_rows = lax.dynamic_slice_in_dim(out_weight, s * piece, piece, 0)
    own_rows = own_rows.reshape(piece, H, quarter).transpose(1, 0, 2)
    own_cols = lax.all_to_all(own_rows, "hid", split_axis=0, concat_axis=0, tiled=True)
    all_cols = lax.all_gather(own_cols, "seq", axis=0, tiled=False)
    out_cols = all_cols.transpose(1, 0, 2, 3).reshape(H * head_rows, quarter)

    grouped = jnp.einsum(
        "ij,bjd->bid", grouping(), patches.reshape(rows // BLOCK, BLOCK, depth),
        preferred_element_type=F32,
    ).astype(BF16).reshape(rows, depth)
    tokens_f = grouped.astype(F32)
    normed_in = (
        tokens_f * lax.rsqrt(jnp.mean(tokens_f * tokens_f, -1, keepdims=True) + 1e-06) * norm_gain
    ).astype(BF16)
    queries = (
        jnp.dot(normed_in, query_weight, preferred_element_type=F32) * HD ** (-0.5)
    ).astype(BF16)
    key_rows = jnp.dot(normed_in, key_weight, preferred_element_type=F32).astype(BF16)
    value_rows = jnp.dot(normed_in, value_weight, preferred_element_type=F32).astype(BF16)

    q_all, k_all, v_all = exchange(queries, key_rows, value_rows, S, L)
    tiles = S * rows // TILE
    ends = jnp.cumsum(tile_counts).astype(jnp.int32)
    tile = jnp.arange(tiles, dtype=jnp.int32)
    after = tile[:, None] >= ends[None, :]
    lo = jnp.max(jnp.where(after, ends[None, :], 0), axis=1).astype(jnp.int32)
    hi = jnp.min(jnp.where(after, tiles, ends[None, :]), axis=1).astype(jnp.int32)
    place = (s % G).astype(jnp.int32).reshape(1)
    heads = attend(q_all, k_all, v_all, lo, hi, place, S, L)
    attended = spread(heads, S, L, H)

    own_tokens = lax.dynamic_slice_in_dim(grouped, h * quarter, quarter, 1)
    own_scale = lax.dynamic_slice_in_dim(layer_scale, h * quarter, quarter, 0)
    merged_normed = merge(
        attended,
        out_cols,
        own_tokens,
        own_scale.reshape(1, quarter),
        merge_gain.reshape(quarter, 4).T,
        merge_bias.reshape(quarter, 4).T,
        S,
        L,
        H,
    )
    partial = jnp.dot(
        merged_normed.reshape(S * rows // 4, 4 * quarter), proj_weight, preferred_element_type=F32
    ).astype(BF16)
    stream_size = image_slots.shape[0] + text_slots.shape[0]
    positions = jnp.arange(stream_size, dtype=jnp.int32)
    chosen = (positions[:, None] == image_slots[None, :]).astype(BF16)
    placed = jnp.dot(chosen, partial, preferred_element_type=F32).astype(BF16)
    share = stream_size // H
    width = partial.shape[1]
    own_positions = h * share + jnp.arange(share, dtype=jnp.int32)
    is_text = own_positions[:, None] == text_slots[None, :]
    text = jnp.dot(is_text.astype(BF16), text_rows, preferred_element_type=F32).astype(BF16)
    is_image = jnp.where(jnp.any(is_text, axis=1, keepdims=True), 0.0, 1.0)
    mask = jnp.broadcast_to(is_image.astype(F32), (share, HD))
    return finish(
        placed.reshape(H, share, width),
        proj_bias.reshape(1, width),
        text,
        mask,
        stream_gain.reshape(1, stream_gain.shape[0]),
        S,
        H,
    )


def solution(mesh):
    return jax.shard_map(
        per_device,
        mesh=mesh,
        in_specs=(
            P("seq", None),
            P(),
            P(None, "hid"),
            P(None, "hid"),
            P(None, "hid"),
            P("hid", None),
            P(),
            P("hid"),
            P("hid"),
            P("hid", "seq"),
            P("seq"),
            P(None, "seq"),
            P("hid"),
            P(),
            P(),
            P(),
        ),
        out_specs=(P("seq", "hid"), P("seq", "hid")),
        check_vma=False,
    )
```

time: 560 us -> 267 us (0.48)
  waiting for transfers between devices: 272 us -> 0.02 us
  Pallas kernels: 0 us -> 185 us
  local copies, waits for them, and re-layouts: 131 us -> 23.9 us
  other arithmetic: 61 us -> 1.39 us
  matrix products: 72.2 us -> 19.1 us
  blocking collectives: 0 us -> 19.3 us
    pallas_call x0 -> x5, Pallas kernels: none -> 185 us  [the longest x1 63.7 us: finish(): pl.pallas_call(functools.partial(finish_kernel, g, H), out_shape=(shape,...]
    psum x2 -> x0, waiting for transfers between devices: 155 us -> none  [the longest x1 98.7 us: per_device(): lax.psum(branch_part.astype(jnp.bfloat16), 'hid').astype(jnp.float32)]
    all_gather x3 -> x1, waiting for transfers between devices: 97.8 us -> 0.01 us  [per_device(): all_cols = lax.all_gather(own_cols, 'seq', axis=0, tiled=False)]
    reshape x4 -> x8, local copies, waits for them, and re-layouts: 78.5 us -> 6.86 us  [the longest x2 2.38 us: per_device(): merge_bias.reshape(quarter, 4)]
    dot_general x17 -> x6, matrix products: 72.2 us -> 19.1 us  [the longest x1 10.9 us: per_device(): placed = jnp.dot(chosen, partial, preferred_element_type=F32).astype(BF16)]
    dynamic_slice x25 -> x3, local copies, waits for them, and re-layouts: 43.7 us -> 2.72 us  [the longest x1 1.17 us: per_device(): own_tokens = lax.dynamic_slice_in_dim(grouped, h * quarter, quarter, 1)]
    reduce_sum x16 -> x0, other arithmetic: 37.4 us -> none  [the longest x1 17.3 us: per_device(): mean_row = jnp.mean(merged, -1, keepdims=True)]
    all_to_all x0 -> x1, blocking collectives: none -> 19.3 us  [per_device(): lax.all_to_all(own_rows, 'hid', split_axis=0, concat_axis=0, tiled=True)]
  transfers between devices with their start and end apart: 6 -> 1, of which waited for: 6 -> 0; matrix products, arithmetic and copies ran while one was open for 2% -> 6% of each run, Pallas kernels for 0% -> 27%
where the time goes in v1:
time: 267 us; the launch traced here: 263 us
  Pallas kernels  185 us (69%)
  local copies, waits for them, and re-layouts  23.9 us (9%)
  blocking collectives  19.3 us (7%)
  matrix products  19.1 us (7%)
  between operations  14.3 us (5%)
    pallas_call x1, Pallas kernels, finish(): pl.pallas_call(functools.partial(finish_kernel, g, H), out_shape=(shape,...  63.7 us
    pallas_call x1, Pallas kernels, merge(): pl.pallas_call(functools.partial(merge_kernel, L, G, H), out_shape=jax.Sh...  50.5 us
    pallas_call x1, Pallas kernels, spread(): pl.pallas_call(functools.partial(spread_kernel, L, S // L, H), out_shape=...  31.4 us
    pallas_call x1, Pallas kernels, exchange(): pl.pallas_call(functools.partial(exchange_kernel, L, G), out_shape=(shape...  27 us
    all_to_all x1, blocking collectives, per_device(): lax.all_to_all(own_rows, 'hid', split_axis=0, concat_axis=0, tiled=True)  19.3 us
    pallas_call x1, Pallas kernels, attend(): pl.pallas_call(functools.partial(attend_kernel, G, rows), out_shape=jax.S...  12.3 us
    dot_general x1, matrix products, per_device(): placed = jnp.dot(chosen, partial, preferred_element_type=F32).astype(BF16)  10.9 us
    unnamed x38, local copies, waits for them, and re-layouts  8.71 us
  transfers between devices with their start and end apart: 1, of which 0 were waited for; matrix products, arithmetic and copies ran while one was open for 6% of the time, Pallas kernels for 27%

profile of v1, /device:TPU:0, one launch (start us, length us, event | category | flops | bytes accessed | tf_op | source)
XLA Modules:
  0.0 263.0 jit_solution(7820871527050832509)
XLA Ops:
  7.2 0.0 copy-start
  7.2 0.0 copy-start.17
  7.2 0.0 copy-start.11
  7.2 0.0 copy-start.10
  7.2 0.0 copy-start.8
  7.2 0.0 copy-start.9
  7.2 0.0 all-gather.3.cloned.1.call-start
  7.3 1.8 copy-done
  9.1 0.8 constant_dynamic-slice_fusion.1
  9.9 2.1 reshape.183
  12.0 1.1 copy.29
  13.1 19.3 %all_to_all.5 = bf16[4,64,800]{2,1,0:T(8,128)(2,1)} all-to-all(bf16[4,64,800]{2,1,0:T(8,128)(2,1)S(1)} %copy.29), channel_id=1, replica_groups=mesh['seq'=8,'hid'=4] {'hid'}, dimensions={0} | all-to-all | bytes 819200 | tf_op jit(solution)/shard_map/all_to_all | solution.py:487
  32.4 0.0 all-gather.3.cloned.1.call-update
  32.4 0.0 copy-done.17
  32.4 0.2 reduce-window.8
  32.6 0.0 copy-done.11
  32.6 0.8 dynamic_slice.11
  33.4 0.0 copy-done.10
  33.4 0.0 copy-done.8
  33.4 0.0 copy-start.7
  33.4 1.2 reshape.186
  34.6 1.2 copy.31
  35.8 0.0 copy-done.9
  35.8 1.2 reshape.187
  37.0 1.2 copy.32
  38.2 2.8 %multiply_reduce_fusion = (f32[3,128]{1,0:T(4,128)S(1)}, bf16[128,3,3200]{2,0,1:T(8,128)(2,1)S(1)}) fusion(bf16[3,128,3200]{2,1,0:T(8,128)(2,1)} %bitcast.46, s32[128]{0:T(128)S(1)} %fusion.10), kind=kOutput, calls=%fused_computation.2 | convolution fusion | flops 319504000 | bytes 4917248 | tf_op jit(solution)/shard_map/ij,bjd->bid/dot_general | solution.py:491
  41.0 0.0 copy-start.13
  41.0 0.0 copy-done.7
  41.0 0.9 multiply_convert_fusion
  41.9 1.0 copy-done.13
  42.9 0.0 copy-start.14
  42.9 1.5 convolution_convert_fusion.2.v_ref
  44.4 0.4 copy-done.14
  44.8 0.0 copy-start.15
  44.8 1.5 convolution_convert_fusion.3.k_ref
  46.3 0.4 copy-done.15
  46.8 1.5 fusion.3.q_ref
  48.2 0.0 copy-start.12
  48.3 27.0 %exchange_heads.1 = (bf16[8,384,128]{2,1,0:T(8,128)(2,1)S(1)}, bf16[8,384,128]{2,1,0:T(8,128)(2,1)S(1)}, bf16[8,384,128]{2,1,0:T(8,128)(2,1)S(1)}) custom-call(bf16[384,512]{1,0:T(8,128)(2,1)S(1)} %fusion.3.q_ref, bf16[384,512]{1,0:T(8,128)(2,1)S(1)} %convolution_convert_fusion.3.k_ref, bf16[384,512]{1,0:T(8,128)(2,1)S(1)} %convolution_convert_fusion.2.v_ref), custom_call_target="tpu_custom_call" | custom-call | tf_op jit(solution)/shard_map/exchange_heads/pallas_call | solution.py:104
  75.3 0.0 copy-start.6
  75.3 0.1 select_reduce_fusion
  75.4 12.3 %attend.1.a_ref = bf16[4,384,128]{2,1,0:T(8,128)(2,1)S(1)} custom-call(s32[3]{0:T(128)S(1)} %get-tuple-element.9.lo, s32[3]{0:T(128)S(1)} %get-tuple-element.8.hi, s32[1]{0:T(128)} %bitcast.2.place, bf16[8,384,128]{2,1,0:T(8,128)(2,1)S(1)} %get-tuple-element.5.q_ref, bf16[3072,128]{1,0:T(8,128)(2,1)S(1)} %bitcast.38, bf16[3072,128]{1,0:T(8,128)(2,1)S(1)} %bitcast.39), custom_call_target="tpu_custom_call" | custom-call | tf_op jit(solution)/shard_map/attend/pallas_call | solution.py:152
  87.7 31.4 %spread_attended.1.a_ref = bf16[384,2048]{1,0:T(8,128)(2,1)S(1)} custom-call(bf16[4,384,128]{2,1,0:T(8,128)(2,1)S(1)} %attend.1.a_ref), custom_call_target="tpu_custom_call" | custom-call | tf_op jit(solution)/shard_map/spread_attended/pallas_call | solution.py:198
  119.1 0.0 copy-start.1
  119.2 1.2 copy-done.1
  120.4 0.0 copy-done.12
  120.4 0.2 compare_reduce_fusion
  120.5 1.2 constant_dynamic-slice_fusion.x_ref
  121.7 0.0 copy-done.6
  121.7 1.0 convolution_convert_fusion.4.text_ref
  122.7 0.0 all-gather.3.cloned.1.call-done
  122.7 4.4 %copy.30 = bf16[4,8,64,800]{3,2,1,0:T(8,128)(2,1)} copy(bf16[4,8,64,800]{3,2,0,1:T(8,128)(2,1)} %bitcast.45) | data formatting | bytes 6553600 | tf_op jit(solution)/shard_map/transpose | solution.py:489
  127.2 0.0 copy-done.2
  127.2 0.0 copy-done.3
  127.2 50.5 %merge_rows.1 = bf16[8,96,3200]{2,1,0:T(8,128)(2,1)} custom-call(bf16[384,2048]{1,0:T(8,128)(2,1)S(1)} %copy-done.2, bf16[2048,800]{1,0:T(8,128)(2,1)} %bitcast.42, bf16[384,800]{1,0:T(8,128)(2,1)S(1)} %copy-done.3, f32[1,800]{1,0:T(1,128)S(1)} %reshape.185.ls_ref, f32[4,800]{1,0:T(4,128)S(1)} %bitcast.40, f32[4,800]{1,0:T(4,128)S(1)} %bitcast.41), custom_call_target="tpu_custom_call" | custom-call | tf_op jit(solution)/shard_map/merge_rows/pallas_call | solution.py:311
  177.7 0.0 copy-done.16
  177.7 10.9 %fusion.1 = bf16[896,768]{1,0:T(8,128)(2,1)} fusion(s32[768]{0:T(1024)S(1)} %copy-done.16, bf16[768,3200]{1,0:T(8,128)(2,1)} %bitcast.44, bf16[3200,768]{1,0:T(8,128)(2,1)} %param.25), kind=kOutput, calls=%fused_computation.5 | convolution fusion | flops 4833804288 | bytes 11209728 | tf_op jit(solution)/shard_map/dot_general | solution.py:535
  188.6 0.1 broadcast_in_dim.34.mask_ref
  188.7 0.0 copy-start.4
  188.7 1.3 copy-done.4
  190.0 1.0 copy-done.5
  191.0 63.7 %finish_rows.1 = (bf16[112,1536]{1,0:T(8,128)(2,1)S(1)}, bf16[112,1536]{1,0:T(8,128)(2,1)S(1)}) custom-call(bf16[4,224,768]{2,1,0:T(8,128)(2,1)S(1)} %bitcast.37, f32[1,768]{1,0:T(1,128)S(1)} %reshape.190.bias_ref, bf16[224,768]{1,0:T(8,128)(2,1)S(1)} %copy-done.5, f32[224,128]{1,0:T(8,128)S(1)} %broadcast_in_dim.34.mask_ref, f32[1,1536]{1,0:T(1,128)S(1)} %reshape.191.gain_ref), custom_call_target="tpu_custom_call" | custom-call | tf_op jit(solution)/shard_map/finish_rows/pallas_call | solution.py:426
  254.7 0.7 copy.35
  255.5 0.7 copy.36
  (11 shorter events, 0.1 us)
Async XLA Ops:
  7.2 1.9 copy-start
  7.2 25.3 %copy-start.17 = (s32[2]{0:T(128)S(1)}, s32[2]{0:T(128)}, u32[]{:S(2)}) copy-start(s32[2]{0:T(128)} %param.29) | copy-start | bytes 28
  7.2 25.4 %copy-start.11 = (f32[768]{0:T(1024)S(1)}, f32[768]{0:T(1024)}, u32[]{:S(2)}) copy-start(f32[768]{0:T(1024)} %param.26) | copy-start | bytes 9220
  7.2 26.2 %copy-start.10 = (f32[1536]{0:T(1024)S(1)}, f32[1536]{0:T(1024)}, u32[]{:S(2)}) copy-start(f32[1536]{0:T(1024)} %param.28) | copy-start | bytes 18436
  7.2 26.2 %copy-start.8 = (f32[3200]{0:T(1024)S(1)}, f32[3200]{0:T(1024)}, u32[]{:S(2)}) copy-start(f32[3200]{0:T(1024)} %param.23) | copy-start | bytes 38404
  7.2 28.6 %copy-start.9 = (f32[3200]{0:T(1024)S(1)}, f32[3200]{0:T(1024)}, u32[]{:S(2)}) copy-start(f32[3200]{0:T(1024)} %param.24) | copy-start | bytes 38404
  7.2 115.5 %all-gather.3.cloned.1.call-start = ((), (), s32[]{:S(2)}) async-start(), calls=%async_computation.1 | async-start | bytes 4128768 | tf_op jit(solution)/shard_map/all_gather | solution.py:488
  33.4 7.6 %copy-start.7 = (f32[3200]{0:T(1024)S(1)}, f32[3200]{0:T(1024)}, u32[]{:S(2)}) copy-start(f32[3200]{0:T(1024)} %param.17) | copy-start | bytes 38404
  41.0 1.9 copy-start.13
  42.9 1.9 copy-start.14
  44.8 1.9 copy-start.15
  48.2 72.1 %copy-start.12 = (s32[128]{0:T(128)S(1)}, s32[128]{0:T(128)}, u32[]{:S(2)}) copy-start(s32[128]{0:T(128)} %param.31) | copy-start | bytes 1540
  75.3 46.4 %copy-start.6 = (bf16[128,768]{1,0:T(8,128)(2,1)S(1)}, bf16[128,768]{1,0:T(8,128)(2,1)}, u32[]{:S(2)}) copy-start(bf16[128,768]{1,0:T(8,128)(2,1)} %param.27) | copy-start | bytes 589828
  119.1 1.2 copy-start.1
  122.7 4.4 %copy-start.2 = (bf16[384,2048]{1,0:T(8,128)(2,1)S(1)}, bf16[384,2048]{1,0:T(8,128)(2,1)}, u32[]{:S(2)}) copy-start(bf16[384,2048]{1,0:T(8,128)(2,1)} %copy-done.1) | copy-start | bytes 4718596
  122.7 4.4 %copy-start.3 = (bf16[384,800]{1,0:T(8,128)(2,1)S(1)}, bf16[384,800]{1,0:T(8,128)(2,1)}, u32[]{:S(2)}) copy-start(bf16[384,800]{1,0:T(8,128)(2,1)} %constant_dynamic-slice_fusion.x_ref) | copy-start | bytes 1843204
  127.2 50.5 %copy-start.16 = (s32[768]{0:T(1024)S(1)}, s32[768]{0:T(1024)}, u32[]{:S(2)}) copy-start(s32[768]{0:T(1024)} %param.30) | copy-start | bytes 9220
  188.7 1.3 copy-start.4
  190.0 1.0 copy-start.5
Sparse Core Ops, SparseCore 0:
  32.5 42.8 all-gather.2

commit v2 on v1

--- a/solution.py
+++ b/solution.py
@@ -46,12 +46,19 @@
     return pl.ds(pl.multiple_of(index * HD, HD), HD)
 
 
-def exchange_kernel(L, G, q_ref, k_ref, v_ref, qo, ko, vo, send1, recv1, send2, recv2):
-    s = lax.axis_index("seq")
+def exchange_kernel(
+    L, G, H, q_ref, k_ref, v_ref, w_ref, qo, ko, vo, wo, send1, recv1, send2, recv2, send3, recv3
+):
+    s, h = lax.axis_index("seq"), lax.axis_index("hid")
     c, k = s // G, s % G
+    planes = [(h + t) % H for t in range(1, H)]
     places = [(c + t) % L for t in range(1, L)]
     mates = [(k + t) % G for t in range(1, G)]
-    greet([{"seq": o * G + k} for o in places] + [{"seq": c * G + m} for m in mates])
+    greet(
+        [{"hid": z} for z in planes]
+        + [{"seq": o * G + k} for o in places]
+        + [{"seq": c * G + m} for m in mates]
+    )
     ins, outs = (k_ref, v_ref, q_ref), (ko, vo, qo)
     sent = []
     for t, o in enumerate(places):
@@ -62,6 +69,11 @@
             )
             copy.start()
             sent.append(copy)
+    for t, z in enumerate(planes):
+        copy = remote(w_ref.at[z], wo.at[h], send3.at[t], recv3.at[h], {"hid": z})
+        copy.start()
+        sent.append(copy)
+    wo[h] = w_ref[h]
     own = head_cols(c)
     for a in range(3):
         outs[a][s] = ins[a][:, own]
@@ -93,28 +105,32 @@
                     outs[a].at[o * G + m], outs[a].at[o * G + m], send2.at[0, 0, a],
                     recv2.at[o, m, a], {"seq": c * G + m},
                 ).wait_recv()
+    for t, z in enumerate(planes):
+        remote(w_ref.at[z], wo.at[z], send3.at[t], recv3.at[z], {"hid": z}).wait_recv()
     for copy in sent:
         copy.wait_send()
 
 
-def exchange(q, k, v, S, L):
+def exchange(q, k, v, w, S, L, H):
     G = S // L
     rows = q.shape[0]
     shape = jax.ShapeDtypeStruct((S, rows, HD), BF16)
     return pl.pallas_call(
-        functools.partial(exchange_kernel, L, G),
-        out_shape=(shape,) * 3,
-        in_specs=[VMEM] * 3,
-        out_specs=(VMEM,) * 3,
+        functools.partial(exchange_kernel, L, G, H),
+        out_shape=(shape,) * 3 + (jax.ShapeDtypeStruct(w.shape, w.dtype),),
+        in_specs=[VMEM] * 4,
+        out_specs=(VMEM,) * 4,
         scratch_shapes=[
             pltpu.SemaphoreType.DMA((L, 3)),
             pltpu.SemaphoreType.DMA((L, 3)),
             pltpu.SemaphoreType.DMA((L, G, 2)),
             pltpu.SemaphoreType.DMA((L, G, 2)),
+            pltpu.SemaphoreType.DMA((H,)),
+            pltpu.SemaphoreType.DMA((H,)),
         ],
         compiler_params=params(0),
         name="exchange_heads",
-    )(q, k, v)
+    )(q, k, v, w)
 
 
 def attend_kernel(G, rows, lo, hi, place, q_ref, k_ref, v_ref, out_ref):
@@ -211,24 +227,36 @@
 
 def merge_kernel(
     L, G, H, a_ref, w_ref, x_ref, ls_ref, gain_ref, bias_ref, out,
-    res, stats, lanes, place, ssend, srecv, send1, recv1, send2, recv2,
+    res, stats, lanes, place, weights, wsem, ssend, srecv, send1, recv1, send2, recv2,
 ):
     s, h = lax.axis_index("seq"), lax.axis_index("hid")
     c, k = s // G, s % G
     planes = [(h + t) % H for t in range(1, H)]
     places = [(c + t) % L for t in range(1, L)]
     mates = [(k + t) % G for t in range(1, G)]
+    piece = w_ref.shape[2]
+    loads = []
+    for z in range(H):
+        for n in range(L * G):
+            at = (z * L * G + n) * piece
+            copy = pltpu.make_async_copy(
+                w_ref.at[n, z], weights.at[at : at + piece], wsem.at[n, z]
+            )
+            copy.start()
+            loads.append(copy)
     greet(
         [{"hid": z} for z in planes]
         + [{"seq": o * G + k} for o in places]
         + [{"seq": c * G + m} for m in mates]
     )
+    for copy in loads:
+        copy.wait()
     rows, width = x_ref.shape
     sub = BLOCK // 4
     full = width // HD
     for b in range(rows // BLOCK):
         span = slice(b * BLOCK, (b + 1) * BLOCK)
-        branch = jnp.dot(a_ref[span, :], w_ref[...], preferred_element_type=F32)
+        branch = jnp.dot(a_ref[span, :], weights[...], preferred_element_type=F32)
         value = x_ref[span, :].astype(F32) + ls_ref[...] * branch
         res[span, :] = value
         one = jnp.sum(value, axis=1, keepdims=True)
@@ -311,13 +339,15 @@
     return pl.pallas_call(
         functools.partial(merge_kernel, L, G, H),
         out_shape=jax.ShapeDtypeStruct((S, rows // 4, 4 * width), BF16),
-        in_specs=[VMEM] * 6,
+        in_specs=[VMEM, pl.BlockSpec(memory_space=pl.ANY)] + [VMEM] * 4,
         out_specs=VMEM,
         scratch_shapes=[
             pltpu.VMEM((rows, width), F32),
             pltpu.VMEM((H, 2, rows // 4, HD), F32),
             pltpu.VMEM((rows // 4, 4 * HD * pl.cdiv(width, HD)), BF16),
             pltpu.VMEM((4 * HD, 4 * HD), BF16),
+            pltpu.VMEM((a.shape[1], width), BF16),
+            pltpu.SemaphoreType.DMA((S, H)),
             pltpu.SemaphoreType.DMA((H,)),
             pltpu.SemaphoreType.DMA((H,)),
             pltpu.SemaphoreType.DMA((L,)),
@@ -331,8 +361,8 @@
 
 
 def finish_kernel(
-    g, H, p_ref, bias_ref, text_ref, mask_ref, gain_ref, stream, normed,
-    parts, rows_out, rows_in, squares, send1, recv1, send2, recv2, send3, recv3,
+    g, H, m_ref, w_ref, slot_ref, bias_ref, text_ref, mask_ref, gain_ref, stream, normed,
+    p_ref, parts, rows_out, rows_in, squares, send1, recv1, send2, recv2, send3, recv3,
 ):
     s, h = lax.axis_index("seq"), lax.axis_index("hid")
     c, k = s // g, s % g
@@ -353,14 +383,33 @@
     pl.semaphore_wait(barrier, len(planes) + g - 1 + off.astype(jnp.int32))
 
     sent = []
-    for t, z in enumerate(planes):
-        copy = remote(p_ref.at[z], parts.at[h], send1.at[t], recv1.at[h], {"hid": z})
-        copy.start()
-        sent.append(copy)
-    for t, z in enumerate(planes):
-        remote(p_ref.at[z], parts.at[z], send1.at[t], recv1.at[z], {"hid": z}).wait_recv()
     part_rows = stream.shape[0]
     width = bias_ref.shape[1]
+    step_rows = 2 * part_rows if g % 2 == 0 else part_rows
+    steps = g * part_rows // step_rows
+
+    def project(t, carry):
+        z = (h + 1 + t) % H
+        for n in range(steps):
+            base = z * (g * part_rows) + n * step_rows
+            position = base + lax.broadcasted_iota(jnp.int32, (step_rows, 1), 0)
+            chosen = jnp.where(position == slot_ref[...], 1.0, 0.0).astype(BF16)
+            rows = jnp.dot(chosen, m_ref[...], preferred_element_type=F32).astype(BF16)
+            p_ref[z, n * step_rows : (n + 1) * step_rows, :] = jnp.dot(
+                rows, w_ref[...], preferred_element_type=F32
+            ).astype(BF16)
+
+        @pl.when(t < H - 1)
+        def _():
+            remote(p_ref.at[z], parts.at[h], send1.at[t], recv1.at[h], {"hid": z}).start()
+
+        return carry
+
+    lax.fori_loop(0, H, project, 0)
+    for t, z in enumerate(planes):
+        copy = remote(p_ref.at[z], parts.at[z], send1.at[t], recv1.at[z], {"hid": z})
+        copy.wait_recv()
+        sent.append(copy)
     for j in range(g):
         span = slice(j * part_rows, (j + 1) * part_rows)
         value = p_ref[h, span, :].astype(F32)
@@ -418,17 +467,18 @@
         copy.wait_send()
 
 
-def finish(placed, bias, text, mask, gain, S, H):
+def finish(merged, weight, slots, bias, text, mask, gain, S, H):
     g = S // H
-    width = placed.shape[-1]
-    part_rows = placed.shape[1] // g
+    width = weight.shape[1]
+    part_rows = text.shape[0] // g
     shape = jax.ShapeDtypeStruct((part_rows, g * width), BF16)
     return pl.pallas_call(
         functools.partial(finish_kernel, g, H),
         out_shape=(shape, shape),
-        in_specs=[VMEM] * 5,
+        in_specs=[VMEM] * 7,
         out_specs=(VMEM, VMEM),
         scratch_shapes=[
+            pltpu.VMEM((H, g * part_rows, width), BF16),
             pltpu.VMEM((H, g * part_rows, width), BF16),
             pltpu.VMEM((g, part_rows, width), BF16),
             pltpu.VMEM((g, part_rows, width), BF16),
@@ -442,7 +492,7 @@
         ],
         compiler_params=params(3),
         name="finish_rows",
-    )(placed, bias, text, mask, gain)
+    )(merged, weight, slots, bias, text, mask, gain)
 
 
 def grouping():
@@ -484,9 +534,6 @@
     piece = head_rows // S
     own_rows = lax.dynamic_slice_in_dim(out_weight, s * piece, piece, 0)
     own_rows = own_rows.reshape(piece, H, quarter).transpose(1, 0, 2)
-    own_cols = lax.all_to_all(own_rows, "hid", split_axis=0, concat_axis=0, tiled=True)
-    all_cols = lax.all_gather(own_cols, "seq", axis=0, tiled=False)
-    out_cols = all_cols.transpose(1, 0, 2, 3).reshape(H * head_rows, quarter)
 
     grouped = jnp.einsum(
         "ij,bjd->bid", grouping(), patches.reshape(rows // BLOCK, BLOCK, depth),
@@ -502,7 +549,10 @@
     key_rows = jnp.dot(normed_in, key_weight, preferred_element_type=F32).astype(BF16)
     value_rows = jnp.dot(normed_in, value_weight, preferred_element_type=F32).astype(BF16)
 
-    q_all, k_all, v_all = exchange(queries, key_rows, value_rows, S, L)
+    q_all, k_all, v_all, own_cols = exchange(
+        queries, key_rows, value_rows, own_rows, S, L, H
+    )
+    out_cols = lax.all_gather(own_cols, "seq", axis=0, tiled=False)
     tiles = S * rows // TILE
     ends = jnp.cumsum(tile_counts).astype(jnp.int32)
     tile = jnp.arange(tiles, dtype=jnp.int32)
@@ -526,22 +576,18 @@
         L,
         H,
     )
-    partial = jnp.dot(
-        merged_normed.reshape(S * rows // 4, 4 * quarter), proj_weight, preferred_element_type=F32
-    ).astype(BF16)
     stream_size = image_slots.shape[0] + text_slots.shape[0]
-    positions = jnp.arange(stream_size, dtype=jnp.int32)
-    chosen = (positions[:, None] == image_slots[None, :]).astype(BF16)
-    placed = jnp.dot(chosen, partial, preferred_element_type=F32).astype(BF16)
     share = stream_size // H
-    width = partial.shape[1]
+    width = proj_weight.shape[1]
     own_positions = h * share + jnp.arange(share, dtype=jnp.int32)
     is_text = own_positions[:, None] == text_slots[None, :]
     text = jnp.dot(is_text.astype(BF16), text_rows, preferred_element_type=F32).astype(BF16)
     is_image = jnp.where(jnp.any(is_text, axis=1, keepdims=True), 0.0, 1.0)
     mask = jnp.broadcast_to(is_image.astype(F32), (share, HD))
     return finish(
-        placed.reshape(H, share, width),
+        merged_normed.reshape(S * rows // 4, 4 * quarter),
+        proj_weight,
+        image_slots.reshape(1, image_slots.shape[0]),
         proj_bias.reshape(1, width),
         text,
         mask,

time: 267 us -> 243 us (0.910)
  blocking collectives: 19.3 us -> 0 us
  matrix products: 19.1 us -> 8.1 us
  local copies, waits for them, and re-layouts: 23.9 us -> 27.8 us
  Pallas kernels: 185 us -> 188 us
    all_to_all x1 -> x0, blocking collectives: 19.3 us -> none  [per_device(): lax.all_to_all(own_rows, 'hid', split_axis=0, concat_axis=0, tiled=True)]
    dot_general x1 -> x0, matrix products: 10.9 us -> none  [per_device(): placed = jnp.dot(chosen, partial, preferred_element_type=F32).astype(BF16)]
    unnamed x38 -> x50, local copies, waits for them, and re-layouts: 8.71 us -> 15.8 us
    transpose x2 -> x0, local copies, waits for them, and re-layouts: 5.49 us -> none  [the longest x1 4.42 us: per_device(): out_cols = all_cols.transpose(1, 0, 2, 3).reshape(H * head_rows, quarter)]
    pallas_call x1, Pallas kernels: 63.7 us -> 68.7 us  [finish(): pl.pallas_call(functools.partial(finish_kernel, g, H), out_shape=(shape,...]
    pallas_call x1, Pallas kernels: 27 us -> 22.5 us  [exchange(): pl.pallas_call(functools.partial(exchange_kernel, L, G, H), out_shape=(sh...]
    pallas_call x1, Pallas kernels: 50.5 us -> 53.6 us  [merge(): pl.pallas_call(functools.partial(merge_kernel, L, G, H), out_shape=jax.Sh...]
  transfers between devices with their start and end apart: 1 -> 1, of which waited for: 0 -> 0; matrix products, arithmetic and copies ran while one was open for 6% -> 4% of each run, Pallas kernels for 27% -> 18%
where the time goes in v2:
time: 243 us; the launch traced here: 239 us
  Pallas kernels  188 us (77%)
  local copies, waits for them, and re-layouts  27.8 us (11%)
  between operations  14.3 us (6%)
  matrix products  8.1 us (3%)
    pallas_call x1, Pallas kernels, finish(): pl.pallas_call(functools.partial(finish_kernel, g, H), out_shape=(shape,...  68.7 us
    pallas_call x1, Pallas kernels, merge(): pl.pallas_call(functools.partial(merge_kernel, L, G, H), out_shape=jax.Sh...  53.6 us
    pallas_call x1, Pallas kernels, spread(): pl.pallas_call(functools.partial(spread_kernel, L, S // L, H), out_shape=...  31.7 us
    pallas_call x1, Pallas kernels, exchange(): pl.pallas_call(functools.partial(exchange_kernel, L, G, H), out_shape=(sh...  22.5 us
    unnamed x50, local copies, waits for them, and re-layouts  15.8 us
    pallas_call x1, Pallas kernels, attend(): pl.pallas_call(functools.partial(attend_kernel, G, rows), out_shape=jax.S...  11.1 us
  transfers between devices with their start and end apart: 1, of which 0 were waited for; matrix products, arithmetic and copies ran while one was open for 4% of the time, Pallas kernels for 18%

profile of v2, /device:TPU:0, one launch (start us, length us, event | category | flops | bytes accessed | tf_op | source)
XLA Modules:
  0.0 239.3 jit_solution(6906471682505498061)
XLA Ops:
  7.2 0.0 copy-start
  7.2 0.0 all-gather.3.cloned.1.call-start
  7.3 1.8 copy-done
  9.1 0.8 constant_dynamic-slice_fusion.1
  9.9 0.0 copy-start.13
  9.9 2.1 reshape.177
  12.0 1.1 copy.28
  13.1 2.6 %multiply_reduce_fusion = (f32[3,128]{1,0:T(4,128)S(1)}, bf16[128,3,3200]{2,0,1:T(8,128)(2,1)S(1)}) fusion(bf16[3,128,3200]{2,1,0:T(8,128)(2,1)} %bitcast.41, s32[128]{0:T(128)S(1)} %fusion.7), kind=kOutput, calls=%fused_computation.2 | convolution fusion | flops 319504000 | bytes 4917248 | tf_op jit(solution)/shard_map/ij,bjd->bid/dot_general | solution.py:538
  15.7 0.0 copy-start.11
  15.7 0.0 copy-start.20
  15.8 0.0 copy-done.13
  15.8 0.9 multiply_convert_fusion
  16.7 1.9 copy-done.20
  18.5 0.0 copy-start.21
  18.5 1.5 convolution_convert_fusion.1.v_ref
  20.1 0.0 copy-done.11
  20.1 0.4 copy-done.21
  20.5 1.5 convolution_convert_fusion.2.k_ref
  22.0 0.4 copy-done.22
  22.4 1.5 fusion.q_ref
  23.9 0.0 copy-start.14
  23.9 22.5 %exchange_heads.1 = (bf16[8,384,128]{2,1,0:T(8,128)(2,1)S(1)}, bf16[8,384,128]{2,1,0:T(8,128)(2,1)S(1)}, bf16[8,384,128]{2,1,0:T(8,128)(2,1)}, bf16[4,64,800]{2,1,0:T(8,128)(2,1)S(1)}) custom-call(bf16[384,512]{1,0:T(8,128)(2,1)S(1)} %fusion.q_ref, bf16[384,512]{1,0:T(8,128)(2,1)S(1)} %convolution_convert_fusion.2.k_ref, ...), custom_call_target="tpu_custom_call" | custom-call | tf_op jit(solution)/shard_map/exchange_heads/pallas_call | solution.py:118
  46.4 0.0 copy-start.5
  46.4 0.9 copy-done.5
  47.3 0.9 copy-done.7
  48.2 0.8 copy-done.10
  49.0 0.0 all-gather.3.cloned.1.call-update
  49.0 0.0 copy-start.16
  49.1 0.0 copy-start.17
  49.1 0.0 copy-start.18
  49.1 0.0 copy-start.19
  49.1 0.0 copy-done.23
  49.1 0.2 reduce-window.8
  49.3 0.1 select_reduce_fusion
  49.4 1.1 copy-done.6
  50.5 1.1 copy-done.8
  51.6 1.1 copy-done.9
  52.8 11.1 %attend.1.a_ref = bf16[4,384,128]{2,1,0:T(8,128)(2,1)S(1)} custom-call(s32[3]{0:T(128)S(1)} %get-tuple-element.11.lo, s32[3]{0:T(128)S(1)} %get-tuple-element.10.hi, s32[1]{0:T(128)} %bitcast.2.place, bf16[8,384,128]{2,1,0:T(8,128)(2,1)S(1)} %copy-done.6, bf16[3072,128]{1,0:T(8,128)(2,1)S(1)} %bitcast.34, bf16[3072,128]{1,0:T(8,128)(2,1)S(1)} %bitcast.35), custom_call_target="tpu_custom_call" | custom-call | tf_op jit(solution)/shard_map/attend/pallas_call | solution.py:168
  63.9 31.7 %spread_attended.1.a_ref = bf16[384,2048]{1,0:T(8,128)(2,1)S(1)} custom-call(bf16[4,384,128]{2,1,0:T(8,128)(2,1)S(1)} %attend.1.a_ref), custom_call_target="tpu_custom_call" | custom-call | tf_op jit(solution)/shard_map/spread_attended/pallas_call | solution.py:214
  95.6 0.0 copy-start.1
  95.6 1.1 copy-done.1
  96.7 0.8 dynamic_slice.11
  97.5 0.0 copy-done.14
  97.5 1.2 reshape.181
  98.8 1.2 copy.25
  99.9 0.0 copy-done.15
  99.9 1.3 reshape.182
  101.2 1.2 copy.26
  102.4 0.0 copy-done.16
  102.4 0.0 copy-done.17
  102.4 0.0 copy-done.18
  102.5 0.0 copy-done.19
  102.5 0.2 compare_reduce_fusion
  102.6 2.4 constant_dynamic-slice_fusion.x_ref
  105.0 0.0 copy-done.12
  105.0 1.0 convolution_convert_fusion.3.text_ref
  106.0 1.4 copy-done.2
  107.5 1.1 copy-done.3
  108.6 53.6 %merge_rows.1 = bf16[8,96,3200]{2,1,0:T(8,128)(2,1)} custom-call(bf16[384,2048]{1,0:T(8,128)(2,1)S(1)} %copy-done.2, bf16[8,4,64,800]{3,2,1,0:T(8,128)(2,1)} %bitcast.40, bf16[384,800]{1,0:T(8,128)(2,1)S(1)} %copy-done.3, f32[1,800]{1,0:T(1,128)S(1)} %reshape.180.ls_ref, f32[4,800]{1,0:T(4,128)S(1)} %bitcast.36, f32[4,800]{1,0:T(4,128)S(1)} %bitcast.37), custom_call_target="tpu_custom_call" | custom-call | tf_op jit(solution)/shard_map/merge_rows/pallas_call | solution.py:339
  162.2 0.1 broadcast_in_dim.48.mask_ref
  162.3 0.0 copy-done.4
  162.3 68.7 %finish_rows.1 = (bf16[112,1536]{1,0:T(8,128)(2,1)S(1)}, bf16[112,1536]{1,0:T(8,128)(2,1)S(1)}) custom-call(bf16[768,3200]{1,0:T(8,128)(2,1)} %bitcast.38, bf16[3200,768]{1,0:T(8,128)(2,1)} %w_ref.1, s32[1,768]{1,0:T(1,128)S(1)} %reshape.184.slot_ref, f32[1,768]{1,0:T(1,128)S(1)} %reshape.185.bias_ref, bf16[224,768]{1,0:T(8,128)(2,1)S(1)} %copy-done.4, ...), custom_call_target="tpu_custom_call" | custom-call | tf_op jit(solution)/shard_map/finish_rows/pallas_call | solution.py:475
  231.0 0.7 copy.31
  231.7 0.7 copy.32
  (21 shorter events, 0.1 us)
Async XLA Ops:
  7.2 1.9 copy-start
  7.2 98.9 %all-gather.3.cloned.1.call-start = ((), (), s32[]{:S(2)}) async-start(), calls=%async_computation | async-start | bytes 4128768 | tf_op jit(solution)/shard_map/all_gather | solution.py:555
  9.9 5.9 %copy-start.13 = (f32[3200]{0:T(1024)S(1)}, f32[3200]{0:T(1024)}, u32[]{:S(2)}) copy-start(f32[3200]{0:T(1024)} %param.17) | copy-start | bytes 38404
  15.7 4.3 %copy-start.11 = (bf16[128,3,3200]{2,0,1:T(8,128)(2,1)}, bf16[128,3,3200]{2,0,1:T(8,128)(2,1)S(1)}, u32[]{:S(2)}) copy-start(bf16[128,3,3200]{2,0,1:T(8,128)(2,1)S(1)} %get-tuple-element.13) | copy-start | bytes 7372804
  15.7 2.8 %copy-start.20 = (bf16[3200,512]{1,0:T(8,128)(2,1)S(1)}, bf16[3200,512]{1,0:T(8,128)(2,1)}, u32[]{:S(2)}) copy-start(bf16[3200,512]{1,0:T(8,128)(2,1)} %param.20) | copy-start | bytes 9830404
  18.5 1.9 copy-start.21
  20.5 1.9 copy-start.22
  22.4 26.7 %copy-start.23 = (s32[2]{0:T(128)S(1)}, s32[2]{0:T(128)}, u32[]{:S(2)}) copy-start(s32[2]{0:T(128)} %param.29) | copy-start | bytes 28
  23.9 73.6 %copy-start.14 = (f32[3200]{0:T(1024)S(1)}, f32[3200]{0:T(1024)}, u32[]{:S(2)}) copy-start(f32[3200]{0:T(1024)} %param.23) | copy-start | bytes 38404
  46.4 0.9 copy-start.5
  47.3 0.9 copy-start.7
  48.2 0.8 copy-start.10
  49.0 50.9 %copy-start.15 = (f32[3200]{0:T(1024)S(1)}, f32[3200]{0:T(1024)}, u32[]{:S(2)}) copy-start(f32[3200]{0:T(1024)} %param.24) | copy-start | bytes 38404
  49.0 53.3 %copy-start.16 = (f32[1536]{0:T(1024)S(1)}, f32[1536]{0:T(1024)}, u32[]{:S(2)}) copy-start(f32[1536]{0:T(1024)} %param.28) | copy-start | bytes 18436
  49.1 53.3 %copy-start.17 = (s32[768]{0:T(1024)S(1)}, s32[768]{0:T(1024)}, u32[]{:S(2)}) copy-start(s32[768]{0:T(1024)} %param.30) | copy-start | bytes 9220
  49.1 53.4 %copy-start.18 = (f32[768]{0:T(1024)S(1)}, f32[768]{0:T(1024)}, u32[]{:S(2)}) copy-start(f32[768]{0:T(1024)} %param.26) | copy-start | bytes 9220
  49.1 53.4 %copy-start.19 = (s32[128]{0:T(128)S(1)}, s32[128]{0:T(128)}, u32[]{:S(2)}) copy-start(s32[128]{0:T(128)} %param.31) | copy-start | bytes 1540
  49.4 1.1 copy-start.6
  50.5 1.1 copy-start.8
  51.6 1.1 copy-start.9
  52.8 52.2 %copy-start.12 = (bf16[128,768]{1,0:T(8,128)(2,1)S(1)}, bf16[128,768]{1,0:T(8,128)(2,1)}, u32[]{:S(2)}) copy-start(bf16[128,768]{1,0:T(8,128)(2,1)} %param.27) | copy-start | bytes 589828
  95.6 1.1 copy-start.1
  106.0 1.4 copy-start.2
  107.5 1.1 copy-start.3
  108.6 53.7 %copy-start.4 = (bf16[224,768]{1,0:T(8,128)(2,1)S(1)}, bf16[224,768]{1,0:T(8,128)(2,1)}, u32[]{:S(2)}) copy-start(bf16[224,768]{1,0:T(8,128)(2,1)} %convolution_convert_fusion.3.text_ref) | copy-start | bytes 1032196
Sparse Core Ops, SparseCore 0:
  49.2 48.5 all-gather.2

commit v3 on v2

--- a/solution.py
+++ b/solution.py
@@ -133,96 +133,92 @@
     )(q, k, v, w)
 
 
-def attend_kernel(G, rows, lo, hi, place, q_ref, k_ref, v_ref, out_ref):
-    first = (pl.program_id(0) * G + place[0]) * rows + pl.program_id(1) * BLOCK
-    tile = lax.div(first, TILE)
-    q = q_ref[0]
-
-    def step(t, carry):
-        top, total, acc = carry
-        span = pl.ds(pl.multiple_of(t * TILE, TILE), TILE)
-        scores = lax.dot_general(
-            q, k_ref[span, :], (((1,), (1,)), ((), ())), preferred_element_type=F32
-        )
-        new_top = jnp.maximum(top, jnp.max(scores, axis=1, keepdims=True))
-        factor = jnp.exp(top - new_top)
-        weights = jnp.exp(scores - new_top)
-        total = total * factor + jnp.sum(weights, axis=1, keepdims=True)
-        acc = acc * factor + jnp.dot(
-            weights.astype(BF16), v_ref[span, :], preferred_element_type=F32
-        )
-        return new_top, total, acc
-
-    start = (
-        jnp.full((BLOCK, 1), -1e30, F32),
-        jnp.zeros((BLOCK, 1), F32),
-        jnp.zeros((BLOCK, HD), F32),
-    )
-    top, total, acc = lax.fori_loop(lo[tile], hi[tile], step, start)
-    out_ref[0] = (acc / total).astype(BF16)
-
-
-def attend(q, k, v, lo, hi, place, S, L):
-    G = S // L
-    rows = q.shape[1]
-    return pl.pallas_call(
-        functools.partial(attend_kernel, G, rows),
-        out_shape=jax.ShapeDtypeStruct((L, rows, HD), BF16),
-        grid_spec=pltpu.PrefetchScalarGridSpec(
-            num_scalar_prefetch=3,
-            grid=(L, rows // BLOCK),
-            in_specs=[
-                pl.BlockSpec((1, BLOCK, HD), lambda a, b, lo, hi, p: (a * G + p[0], b, 0)),
-                VMEM,
-                VMEM,
-            ],
-            out_specs=pl.BlockSpec((1, BLOCK, HD), lambda a, b, lo, hi, p: (a, b, 0)),
-        ),
-        compiler_params=pltpu.CompilerParams(vmem_limit_bytes=LIMIT),
-        name="attend",
-    )(lo, hi, place, q, k.reshape(S * rows, HD), v.reshape(S * rows, HD))
-
-
-def spread_kernel(L, G, H, a_ref, out, send, recv):
+def attend_kernel(
+    L, G, H, tiles, q_ref, k_ref, v_ref, bias_ref, out, heads, send, recv
+):
     s, h = lax.axis_index("seq"), lax.axis_index("hid")
     c, k = s // G, s % G
+    rows = heads.shape[1]
     peers = [
-        ((c + dc) % L, (h + dh) % H) for dh in range(H) for dc in range(L) if dc or dh
+        ((c + dc) % L, (h + dh) % H)
+        for dc in (*range(1, L), 0)
+        for dh in (*range(1, H), 0)
+        if dc or dh
     ]
     ids = [{"seq": o * G + k, "hid": z} for o, z in peers]
     greet(ids)
     mine = h * L + c
     sent = []
-    for t, (o, z) in enumerate(peers):
-        copy = remote(
-            a_ref.at[o], out.at[:, head_cols(mine)], send.at[t], recv.at[mine], ids[t]
-        )
-        copy.start()
-        sent.append(copy)
-    out[:, head_cols(mine)] = a_ref[c]
+    for n in range(L):
+        o = (c + n + 1) % L
+        slot = o * G + k
+
+        def block(i, carry):
+            at = pl.multiple_of(i * BLOCK, BLOCK)
+            tile = (slot * rows + i * BLOCK) // TILE
+            q = q_ref[slot, pl.ds(at, BLOCK), :]
+
+            def step(t, state):
+                top, total, acc = state
+                span = pl.ds(pl.multiple_of(t * TILE, TILE), TILE)
+                scores = lax.dot_general(
+                    q, k_ref[span, :], (((1,), (1,)), ((), ())), preferred_element_type=F32
+                )
+                scores = scores + bias_ref[tile * tiles + t][:, :1]
+                new_top = jnp.maximum(top, jnp.max(scores, axis=1, keepdims=True))
+                factor = jnp.exp(top - new_top)
+                weights = jnp.exp(scores - new_top)
+                total = total * factor + jnp.sum(weights, axis=1, keepdims=True)
+                acc = acc * factor + jnp.dot(
+                    weights.astype(BF16), v_ref[span, :], preferred_element_type=F32
+                )
+                return new_top, total, acc
+
+            state = (
+                jnp.full((BLOCK, 1), -1e30, F32),
+                jnp.zeros((BLOCK, 1), F32),
+                jnp.zeros((BLOCK, HD), F32),
+            )
+            if tiles <= 4:
+                for t in range(tiles):
+                    state = step(t, state)
+            else:
+                state = lax.fori_loop(0, tiles, step, state)
+            heads[o, pl.ds(at, BLOCK), :] = (state[2] / state[1]).astype(BF16)
+            return carry
+
+        lax.fori_loop(0, rows // BLOCK, block, 0)
+        for t in range(n * H, min((n + 1) * H, len(peers))):
+            copy = remote(
+                heads.at[o], out.at[:, head_cols(mine)], send.at[t], recv.at[mine], ids[t]
+            )
+            copy.start()
+            sent.append(copy)
+    out[:, head_cols(mine)] = heads[c]
     for t, (o, z) in enumerate(peers):
         source = z * L + o
         remote(
-            a_ref.at[o], out.at[:, head_cols(source)], send.at[t], recv.at[source], ids[t]
+            heads.at[o], out.at[:, head_cols(source)], send.at[t], recv.at[source], ids[t]
         ).wait_recv()
     for copy in sent:
         copy.wait_send()
 
 
-def spread(a, S, L, H):
-    rows = a.shape[1]
+def attend(q, k, v, bias, S, L, H):
+    rows = q.shape[1]
     return pl.pallas_call(
-        functools.partial(spread_kernel, L, S // L, H),
+        functools.partial(attend_kernel, L, S // L, H, S * rows // TILE),
         out_shape=jax.ShapeDtypeStruct((rows, H * L * HD), BF16),
-        in_specs=[VMEM],
+        in_specs=[VMEM] * 4,
         out_specs=VMEM,
         scratch_shapes=[
+            pltpu.VMEM((L, rows, HD), BF16),
             pltpu.SemaphoreType.DMA((H * L,)),
             pltpu.SemaphoreType.DMA((H * L,)),
         ],
         compiler_params=params(1),
-        name="spread_attended",
-    )(a)
+        name="attend_and_spread",
+    )(q, k.reshape(S * rows, HD), v.reshape(S * rows, HD), bias)
 
 
 def merge_kernel(
@@ -388,63 +384,83 @@
     step_rows = 2 * part_rows if g % 2 == 0 else part_rows
     steps = g * part_rows // step_rows
 
+    def part(j):
+        return slice(j * part_rows, (j + 1) * part_rows)
+
+    def first_send(t, z, j):
+        return remote(
+            p_ref.at[z, part(j)], parts.at[h, part(j)], send1.at[t, j], recv1.at[h, j], {"hid": z}
+        )
+
     def project(t, carry):
         z = (h + 1 + t) % H
-        for n in range(steps):
-            base = z * (g * part_rows) + n * step_rows
+
+        def some(n, inner):
+            at = n * step_rows
+            base = z * (g * part_rows) + at
             position = base + lax.broadcasted_iota(jnp.int32, (step_rows, 1), 0)
             chosen = jnp.where(position == slot_ref[...], 1.0, 0.0).astype(BF16)
             rows = jnp.dot(chosen, m_ref[...], preferred_element_type=F32).astype(BF16)
-            p_ref[z, n * step_rows : (n + 1) * step_rows, :] = jnp.dot(
-                rows, w_ref[...], preferred_element_type=F32
-            ).astype(BF16)
+            value = jnp.dot(rows, w_ref[...], preferred_element_type=F32).astype(BF16)
+            if steps == 1:
+                p_ref[z] = value
+            else:
+                p_ref[z, pl.ds(pl.multiple_of(at, step_rows), step_rows), :] = value
+            return inner
+
+        if steps == 1:
+            some(0, 0)
+        else:
+            lax.fori_loop(0, steps, some, 0)
 
         @pl.when(t < H - 1)
         def _():
-            remote(p_ref.at[z], parts.at[h], send1.at[t], recv1.at[h], {"hid": z}).start()
+            first_send(t, z, 0).start()
 
         return carry
 
     lax.fori_loop(0, H, project, 0)
-    for t, z in enumerate(planes):
-        copy = remote(p_ref.at[z], parts.at[z], send1.at[t], recv1.at[z], {"hid": z})
-        copy.wait_recv()
-        sent.append(copy)
+    for j in range(1, g):
+        for t, z in enumerate(planes):
+            first_send(t, z, j).start()
     for j in range(g):
-        span = slice(j * part_rows, (j + 1) * part_rows)
+        span = part(j)
         value = p_ref[h, span, :].astype(F32)
-        for z in planes:
+        for t, z in enumerate(planes):
+            copy = remote(
+                p_ref.at[z, span], parts.at[z, span], send1.at[t, j], recv1.at[z, j], {"hid": z}
+            )
+            copy.wait_recv()
+            sent.append(copy)
             value = value + parts[z, span, :].astype(F32)
         value = value + bias_ref[...]
         value = value * (lax.erf(value * F32(0.7071067811865476)) + 1.0) * 0.5
         rows_out[j] = jnp.where(
             mask_ref[span, :1] > 0.5, value, text_ref[span, :].astype(F32)
         ).astype(BF16)
-    for t in range(g):
-        j = (k + t) % g
-        partner = {"seq": g * h + j, "hid": c}
-        copy = remote(rows_out.at[j], rows_in.at[k], send2.at[t], recv2.at[k], partner)
-        if t:
-            copy.start()
-            sent.append(copy)
-        else:
-            pl.when(off)(copy.start)
-
-            @pl.when(jnp.logical_not(off))
-            def _():
-                rows_in[k] = rows_out[k]
-
-    for t in range(g):
-        j = (k + t) % g
-        partner = {"seq": g * h + j, "hid": c}
-        copy = remote(rows_out.at[j], rows_in.at[j], send2.at[t], recv2.at[j], partner)
-        if t:
+        away = jnp.logical_or(off, k != j)
+
+        @pl.when(away)
+        def _():
+            remote(
+                rows_out.at[j], rows_in.at[k], send2.at[j], recv2.at[k],
+                {"seq": g * h + j, "hid": c},
+            ).start()
+
+        @pl.when(jnp.logical_not(away))
+        def _():
+            rows_in[k] = rows_out[j]
+
+    for j in range(g):
+        @pl.when(jnp.logical_or(off, k != j))
+        def _():
+            copy = remote(
+                rows_out.at[j], rows_in.at[j], send2.at[j], recv2.at[j],
+                {"seq": g * h + j, "hid": c},
+            )
             copy.wait_recv()
-        else:
-            @pl.when(off)
-            def _():
-                copy.wait_recv()
-                copy.wait_send()
+            copy.wait_send()
+
     square = jnp.zeros((part_rows, 1), F32)
     for j in range(g):
         value = rows_in[j]
@@ -483,8 +499,8 @@
             pltpu.VMEM((g, part_rows, width), BF16),
             pltpu.VMEM((g, part_rows, width), BF16),
             pltpu.VMEM((H, part_rows, HD), F32),
-            pltpu.SemaphoreType.DMA((H,)),
-            pltpu.SemaphoreType.DMA((H,)),
+            pltpu.SemaphoreType.DMA((H, g)),
+            pltpu.SemaphoreType.DMA((H, g)),
             pltpu.SemaphoreType.DMA((g,)),
             pltpu.SemaphoreType.DMA((g,)),
             pltpu.SemaphoreType.DMA((H,)),
@@ -556,12 +572,10 @@
     tiles = S * rows // TILE
     ends = jnp.cumsum(tile_counts).astype(jnp.int32)
     tile = jnp.arange(tiles, dtype=jnp.int32)
-    after = tile[:, None] >= ends[None, :]
-    lo = jnp.max(jnp.where(after, ends[None, :], 0), axis=1).astype(jnp.int32)
-    hi = jnp.min(jnp.where(after, tiles, ends[None, :]), axis=1).astype(jnp.int32)
-    place = (s % G).astype(jnp.int32).reshape(1)
-    heads = attend(q_all, k_all, v_all, lo, hi, place, S, L)
-    attended = spread(heads, S, L, H)
+    image = jnp.sum((tile[:, None] >= ends[None, :]).astype(jnp.int32), axis=1)
+    bias = jnp.where(image[:, None] == image[None, :], 0.0, -1e30).astype(F32)
+    bias = jnp.broadcast_to(bias.reshape(tiles * tiles, 1, 1), (tiles * tiles, 1, HD))
+    attended = attend(q_all, k_all, v_all, bias, S, L, H)
 
     own_tokens = lax.dynamic_slice_in_dim(grouped, h * quarter, quarter, 1)
     own_scale = lax.dynamic_slice_in_dim(layer_scale, h * quarter, quarter, 0)

time: 243 us -> 230 us (0.947); the launches traced: 239 us -> 229 us
  Pallas kernels: 188 us -> 177 us
    pallas_call x1, Pallas kernels: 53.6 us -> 46.9 us  [merge(): pl.pallas_call(functools.partial(merge_kernel, L, G, H), out_shape=jax.Sh...]
    pallas_call x2 -> x1, Pallas kernels: 42.8 us -> 40.9 us  [attend(): pl.pallas_call(functools.partial(attend_kernel, L, S // L, H, S * rows //...]
where the time goes in v3:
time: 230 us; the launch traced here: 229 us
  Pallas kernels  177 us (77%)
  local copies, waits for them, and re-layouts  28 us (12%)
  between operations  14.3 us (6%)
  matrix products  8.12 us (4%)
    pallas_call x1, Pallas kernels, finish(): pl.pallas_call(functools.partial(finish_kernel, g, H), out_shape=(shape,...  67.1 us
    pallas_call x1, Pallas kernels, merge(): pl.pallas_call(functools.partial(merge_kernel, L, G, H), out_shape=jax.Sh...  46.9 us
    pallas_call x1, Pallas kernels, attend(): pl.pallas_call(functools.partial(attend_kernel, L, S // L, H, S * rows //...  40.9 us
    pallas_call x1, Pallas kernels, exchange(): pl.pallas_call(functools.partial(exchange_kernel, L, G, H), out_shape=(sh...  22.5 us
    unnamed x50, local copies, waits for them, and re-layouts  15.8 us
  transfers between devices with their start and end apart: 1, of which 0 were waited for; matrix products, arithmetic and copies ran while one was open for 4% of the time, Pallas kernels for 18%

profile of v3, /device:TPU:0, one launch (start us, length us, event | category | flops | bytes accessed | tf_op | source)
XLA Modules:
  0.0 229.3 jit_solution(16244633089892554564)
XLA Ops:
  7.2 0.0 copy-start
  7.2 0.0 all-gather.3.cloned.1.call-start
  7.3 1.8 copy-done
  9.1 0.8 constant_dynamic-slice_fusion.1
  9.9 0.0 copy-start.13
  9.9 2.1 reshape.194
  12.0 1.1 copy.28
  13.1 2.6 %multiply_reduce_fusion = (f32[3,128]{1,0:T(4,128)S(1)}, bf16[128,3,3200]{2,0,1:T(8,128)(2,1)S(1)}) fusion(bf16[3,128,3200]{2,1,0:T(8,128)(2,1)} %bitcast.40, s32[128]{0:T(128)S(1)} %fusion.8), kind=kOutput, calls=%fused_computation.2 | convolution fusion | flops 319504000 | bytes 4917248 | tf_op jit(solution)/shard_map/ij,bjd->bid/dot_general | solution.py:554
  15.7 0.0 copy-start.11
  15.7 0.0 copy-start.20
  15.8 0.0 copy-done.13
  15.8 0.9 multiply_convert_fusion
  16.7 1.9 copy-done.20
  18.5 0.0 copy-start.21
  18.5 1.5 convolution_convert_fusion.1.v_ref
  20.1 0.0 copy-done.11
  20.1 0.4 copy-done.21
  20.5 1.5 convolution_convert_fusion.2.k_ref
  22.0 0.4 copy-done.22
  22.4 1.5 fusion.q_ref
  23.9 0.0 copy-start.16
  23.9 0.0 copy-start.17
  23.9 0.0 copy-start.18
  23.9 22.5 %exchange_heads.1 = (bf16[8,384,128]{2,1,0:T(8,128)(2,1)S(1)}, bf16[8,384,128]{2,1,0:T(8,128)(2,1)S(1)}, bf16[8,384,128]{2,1,0:T(8,128)(2,1)}, bf16[4,64,800]{2,1,0:T(8,128)(2,1)S(1)}) custom-call(bf16[384,512]{1,0:T(8,128)(2,1)S(1)} %fusion.q_ref, bf16[384,512]{1,0:T(8,128)(2,1)S(1)} %convolution_convert_fusion.2.k_ref, ...), custom_call_target="tpu_custom_call" | custom-call | tf_op jit(solution)/shard_map/exchange_heads/pallas_call | solution.py:118
  46.4 0.0 copy-start.5
  46.4 0.9 copy-done.5
  47.4 0.9 copy-done.7
  48.3 0.8 copy-done.10
  49.1 0.0 all-gather.3.cloned.1.call-update
  49.1 0.0 copy-done.23
  49.1 0.2 reduce-window.8
  49.3 0.1 fusion.7
  49.4 0.1 compare_select_fusion
  49.5 0.1 select_n.85
  49.5 0.8 dynamic_slice.11
  50.3 0.0 copy-done.14
  50.3 1.2 reshape.200
  51.5 1.2 copy.25
  52.8 0.0 copy-done.15
  52.8 1.2 reshape.201
  54.0 1.2 copy.26
  55.2 0.0 copy-done.16
  55.2 0.0 copy-done.17
  55.2 0.0 copy-done.18
  55.3 0.1 broadcast_in_dim.22.bias_ref
  55.3 1.2 copy-done.6
  56.5 1.1 copy-done.8
  57.6 1.1 copy-done.9
  58.8 40.9 %attend_and_spread.1.a_ref = bf16[384,2048]{1,0:T(8,128)(2,1)S(1)} custom-call(bf16[8,384,128]{2,1,0:T(8,128)(2,1)S(1)} %copy-done.6, bf16[3072,128]{1,0:T(8,128)(2,1)S(1)} %bitcast.33, bf16[3072,128]{1,0:T(8,128)(2,1)S(1)} %bitcast.34, f32[9,1,128]{2,1,0:T(1,128)S(1)} %broadcast_in_dim.22.bias_ref), custom_call_target="tpu_custom_call" | custom-call | tf_op jit(solution)/shard_map/attend_and_spread/pallas_call | solution.py:209
  99.6 0.0 copy-start.1
  99.7 1.1 copy-done.1
  100.8 0.0 copy-done.19
  100.8 0.2 compare_reduce_fusion
  101.0 2.4 %constant_dynamic-slice_fusion.x_ref = bf16[384,800]{1,0:T(8,128)(2,1)} fusion(bf16[384,3200]{1,0:T(8,128)(2,1)} %bitcast.38, s32[]{:T(128)S(6)} %select_n.86), kind=kLoop, calls=%fused_computation.40 | loop fusion | bytes 1228804 | tf_op jit(solution)/shard_map/dynamic_slice | solution.py:580
  103.3 0.0 copy-done.12
  103.3 1.0 convolution_convert_fusion.3.text_ref
  104.4 1.4 copy-done.2
  105.8 1.1 copy-done.3
  106.9 46.9 %merge_rows.1 = bf16[8,96,3200]{2,1,0:T(8,128)(2,1)} custom-call(bf16[384,2048]{1,0:T(8,128)(2,1)S(1)} %copy-done.2, bf16[8,4,64,800]{3,2,1,0:T(8,128)(2,1)} %bitcast.39, bf16[384,800]{1,0:T(8,128)(2,1)S(1)} %copy-done.3, f32[1,800]{1,0:T(1,128)S(1)} %reshape.199.ls_ref, f32[4,800]{1,0:T(4,128)S(1)} %bitcast.35, f32[4,800]{1,0:T(4,128)S(1)} %bitcast.36), custom_call_target="tpu_custom_call" | custom-call | tf_op jit(solution)/shard_map/merge_rows/pallas_call | solution.py:335
  153.8 0.1 broadcast_in_dim.42.mask_ref
  153.9 0.0 copy-done.4
  153.9 67.1 %finish_rows.1 = (bf16[112,1536]{1,0:T(8,128)(2,1)S(1)}, bf16[112,1536]{1,0:T(8,128)(2,1)S(1)}) custom-call(bf16[768,3200]{1,0:T(8,128)(2,1)} %bitcast.37, bf16[3200,768]{1,0:T(8,128)(2,1)} %w_ref.1, s32[1,768]{1,0:T(1,128)S(1)} %reshape.203.slot_ref, f32[1,768]{1,0:T(1,128)S(1)} %reshape.204.bias_ref, bf16[224,768]{1,0:T(8,128)(2,1)S(1)} %copy-done.4, ...), custom_call_target="tpu_custom_call" | custom-call | tf_op jit(solution)/shard_map/finish_rows/pallas_call | solution.py:491
  221.0 0.7 copy.31
  221.7 0.7 copy.32
  (23 shorter events, 0.1 us)
Async XLA Ops:
  7.2 1.9 copy-start
  7.2 97.2 %all-gather.3.cloned.1.call-start = ((), (), s32[]{:S(2)}) async-start(), calls=%async_computation | async-start | bytes 4128768 | tf_op jit(solution)/shard_map/all_gather | solution.py:571
  9.9 5.9 %copy-start.13 = (f32[3200]{0:T(1024)S(1)}, f32[3200]{0:T(1024)}, u32[]{:S(2)}) copy-start(f32[3200]{0:T(1024)} %param.17) | copy-start | bytes 38404
  15.7 4.3 %copy-start.11 = (bf16[128,3,3200]{2,0,1:T(8,128)(2,1)}, bf16[128,3,3200]{2,0,1:T(8,128)(2,1)S(1)}, u32[]{:S(2)}) copy-start(bf16[128,3,3200]{2,0,1:T(8,128)(2,1)S(1)} %get-tuple-element.11) | copy-start | bytes 7372804
  15.7 2.8 %copy-start.20 = (bf16[3200,512]{1,0:T(8,128)(2,1)S(1)}, bf16[3200,512]{1,0:T(8,128)(2,1)}, u32[]{:S(2)}) copy-start(bf16[3200,512]{1,0:T(8,128)(2,1)} %param.20) | copy-start | bytes 9830404
  18.5 1.9 copy-start.21
  20.5 1.9 copy-start.22
  22.4 26.7 %copy-start.23 = (s32[2]{0:T(128)S(1)}, s32[2]{0:T(128)}, u32[]{:S(2)}) copy-start(s32[2]{0:T(128)} %param.29) | copy-start | bytes 28
  22.4 27.9 %copy-start.14 = (f32[3200]{0:T(1024)S(1)}, f32[3200]{0:T(1024)}, u32[]{:S(2)}) copy-start(f32[3200]{0:T(1024)} %param.23) | copy-start | bytes 38404
  22.4 30.4 %copy-start.15 = (f32[3200]{0:T(1024)S(1)}, f32[3200]{0:T(1024)}, u32[]{:S(2)}) copy-start(f32[3200]{0:T(1024)} %param.24) | copy-start | bytes 38404
  23.9 31.3 %copy-start.16 = (f32[1536]{0:T(1024)S(1)}, f32[1536]{0:T(1024)}, u32[]{:S(2)}) copy-start(f32[1536]{0:T(1024)} %param.28) | copy-start | bytes 18436
  23.9 31.3 %copy-start.17 = (s32[768]{0:T(1024)S(1)}, s32[768]{0:T(1024)}, u32[]{:S(2)}) copy-start(s32[768]{0:T(1024)} %param.30) | copy-start | bytes 9220
  23.9 31.3 %copy-start.18 = (f32[768]{0:T(1024)S(1)}, f32[768]{0:T(1024)}, u32[]{:S(2)}) copy-start(f32[768]{0:T(1024)} %param.26) | copy-start | bytes 9220
  46.4 0.9 copy-start.5
  47.4 0.9 copy-start.7
  48.3 0.8 copy-start.10
  49.1 51.7 %copy-start.19 = (s32[128]{0:T(128)S(1)}, s32[128]{0:T(128)}, u32[]{:S(2)}) copy-start(s32[128]{0:T(128)} %param.31) | copy-start | bytes 1540
  51.5 51.8 %copy-start.12 = (bf16[128,768]{1,0:T(8,128)(2,1)S(1)}, bf16[128,768]{1,0:T(8,128)(2,1)}, u32[]{:S(2)}) copy-start(bf16[128,768]{1,0:T(8,128)(2,1)} %param.27) | copy-start | bytes 589828
  55.3 1.2 copy-start.6
  56.5 1.1 copy-start.8
  57.6 1.1 copy-start.9
  99.6 1.2 copy-start.1
  104.4 1.4 copy-start.2
  105.8 1.1 copy-start.3
  106.9 47.0 %copy-start.4 = (bf16[224,768]{1,0:T(8,128)(2,1)S(1)}, bf16[224,768]{1,0:T(8,128)(2,1)}, u32[]{:S(2)}) copy-start(bf16[224,768]{1,0:T(8,128)(2,1)} %convolution_convert_fusion.3.text_ref) | copy-start | bytes 1032196
Sparse Core Ops, SparseCore 0:
  49.2 46.4 all-gather.2

commit v4 on v3

--- a/solution.py
+++ b/solution.py
@@ -222,8 +222,8 @@
 
 
 def merge_kernel(
-    L, G, H, a_ref, w_ref, x_ref, ls_ref, gain_ref, bias_ref, out,
-    res, stats, lanes, place, weights, wsem, ssend, srecv, send1, recv1, send2, recv2,
+    L, G, H, a_ref, w_ref, x_ref, ls_ref, affine_ref, out,
+    res, stats, lanes, affine, place, weights, wsem, ssend, srecv, send1, recv1, send2, recv2,
 ):
     s, h = lax.axis_index("seq"), lax.axis_index("hid")
     c, k = s // G, s % G
@@ -269,6 +269,17 @@
     row = lax.broadcasted_iota(jnp.int32, (4 * HD, 4 * HD), 0)
     col = lax.broadcasted_iota(jnp.int32, (4 * HD, 4 * HD), 1)
     place[...] = jnp.where(col == 4 * (row % HD) + lax.div(row, HD), 1.0, 0.0).astype(BF16)
+    for j in range(pl.cdiv(width, HD)):
+        cols = slice(4 * j * HD, 4 * (j + 1) * HD)
+        rest = affine_ref[:, cols]
+        total = jnp.zeros_like(rest)
+        for _ in range(3):
+            term = rest.astype(BF16)
+            rest = rest - term.astype(F32)
+            total = total + lax.dot_general(
+                term, place[...], (((1,), (1,)), ((), ())), preferred_element_type=F32
+            )
+        affine[:, cols] = total
     for t, z in enumerate(planes):
         remote(stats.at[z], stats.at[z], ssend.at[t], srecv.at[z], {"hid": z}).wait_recv()
     total = stats[0]
@@ -283,12 +294,12 @@
         for q in range(4):
             start = b * BLOCK + q * sub
             value = (res[start : start + sub, :] - mean_b) * scale_b
-            value = (value * gain_ref[q : q + 1, :] + bias_ref[q : q + 1, :]).astype(BF16)
-            for j in range(full):
-                lanes[part, (4 * j + q) * HD : (4 * j + q + 1) * HD] = value[:, j * HD : (j + 1) * HD]
-            if width % HD:
-                at = (4 * full + q) * HD
-                lanes[part, at : at + width % HD] = value[:, full * HD :]
+            for j in range(pl.cdiv(width, HD)):
+                size = min(HD, width - j * HD)
+                at = (4 * j + q) * HD
+                part_value = value[:, j * HD : j * HD + size]
+                part_value = part_value * affine[0:1, at : at + size] + affine[1:2, at : at + size]
+                lanes[part, at : at + size] = part_value.astype(BF16)
     for j in range(full):
         cols = slice(4 * j * HD, 4 * (j + 1) * HD)
         out[s, :, cols] = jnp.dot(
@@ -329,18 +340,19 @@
         copy.wait_send()
 
 
-def merge(a, w, x, ls, gain, bias, S, L, H):
+def merge(a, w, x, ls, affine, S, L, H):
     G = S // L
     rows, width = x.shape
     return pl.pallas_call(
         functools.partial(merge_kernel, L, G, H),
         out_shape=jax.ShapeDtypeStruct((S, rows // 4, 4 * width), BF16),
-        in_specs=[VMEM, pl.BlockSpec(memory_space=pl.ANY)] + [VMEM] * 4,
+        in_specs=[VMEM, pl.BlockSpec(memory_space=pl.ANY)] + [VMEM] * 3,
         out_specs=VMEM,
         scratch_shapes=[
             pltpu.VMEM((rows, width), F32),
             pltpu.VMEM((H, 2, rows // 4, HD), F32),
             pltpu.VMEM((rows // 4, 4 * HD * pl.cdiv(width, HD)), BF16),
+            pltpu.VMEM(affine.shape, F32),
             pltpu.VMEM((4 * HD, 4 * HD), BF16),
             pltpu.VMEM((a.shape[1], width), BF16),
             pltpu.SemaphoreType.DMA((S, H)),
@@ -353,7 +365,7 @@
         ],
         compiler_params=params(2),
         name="merge_rows",
-    )(a, w, x, ls, gain, bias)
+    )(a, w, x, ls, affine)
 
 
 def finish_kernel(
@@ -549,7 +561,9 @@
     head_rows = out_weight.shape[0]
     piece = head_rows // S
     own_rows = lax.dynamic_slice_in_dim(out_weight, s * piece, piece, 0)
-    own_rows = own_rows.reshape(piece, H, quarter).transpose(1, 0, 2)
+    own_rows = jnp.stack(
+        [own_rows[:, z * quarter : (z + 1) * quarter] for z in range(H)]
+    )
 
     grouped = jnp.einsum(
         "ij,bjd->bid", grouping(), patches.reshape(rows // BLOCK, BLOCK, depth),
@@ -579,13 +593,14 @@
 
     own_tokens = lax.dynamic_slice_in_dim(grouped, h * quarter, quarter, 1)
     own_scale = lax.dynamic_slice_in_dim(layer_scale, h * quarter, quarter, 0)
+    padding = 4 * HD * pl.cdiv(quarter, HD) - 4 * quarter
+    affine = jnp.pad(jnp.stack([merge_gain, merge_bias]), ((0, 6), (0, padding)))
     merged_normed = merge(
         attended,
         out_cols,
         own_tokens,
         own_scale.reshape(1, quarter),
-        merge_gain.reshape(quarter, 4).T,
-        merge_bias.reshape(quarter, 4).T,
+        affine,
         S,
         L,
         H,

time: 230 us -> 223 us (0.970)
  local copies, waits for them, and re-layouts: 28 us -> 18.9 us
  matrix products: 8.12 us -> 10.5 us
    reshape x6 -> x0, local copies, waits for them, and re-layouts: 8.06 us -> none  [the longest x2 3.21 us: per_device(): own_rows = own_rows.reshape(piece, H, quarter).transpose(1, 0, 2)]
    unnamed x50 -> x54, local copies, waits for them, and re-layouts: 15.8 us -> 14.2 us
  transfers between devices with their start and end apart: 1 -> 1, of which waited for: 0 -> 0; matrix products, arithmetic and copies ran while one was open for 4% -> 2% of each run, Pallas kernels for 18% -> 18%
where the time goes in v4:
time: 223 us
  Pallas kernels  177 us (79%)
  local copies, waits for them, and re-layouts  18.9 us (8%)
  between operations  14.3 us (6%)
  matrix products  10.5 us (5%)
    pallas_call x1, Pallas kernels, finish(): pl.pallas_call(functools.partial(finish_kernel, g, H), out_shape=(shape,...  66.2 us
    pallas_call x1, Pallas kernels, merge(): pl.pallas_call(functools.partial(merge_kernel, L, G, H), out_shape=jax.Sh...  47.7 us
    pallas_call x1, Pallas kernels, attend(): pl.pallas_call(functools.partial(attend_kernel, L, S // L, H, S * rows //...  41 us
    pallas_call x1, Pallas kernels, exchange(): pl.pallas_call(functools.partial(exchange_kernel, L, G, H), out_shape=(sh...  22.4 us
    unnamed x54, local copies, waits for them, and re-layouts  14.2 us
  transfers between devices with their start and end apart: 1, of which 0 were waited for; matrix products, arithmetic and copies ran while one was open for 2% of the time, Pallas kernels for 18%

profile of v4, /device:TPU:0, one launch (start us, length us, event | category | flops | bytes accessed | tf_op | source)
XLA Modules:
  0.0 222.7 jit_solution(18381037632979473944)
XLA Ops:
  7.2 0.0 copy-start
  7.2 0.0 copy-start.16
  7.2 0.0 all-gather.3.cloned.1.call-start
  7.3 2.8 %multiply_reduce_fusion = (f32[3,128]{1,0:T(4,128)S(1)}, bf16[128,3,3200]{2,0,1:T(8,128)(2,1)S(1)}) fusion(bf16[3,128,3200]{2,1,0:T(8,128)(2,1)} %bitcast.40, s32[128]{0:T(128)S(1)} %fusion.8), kind=kOutput, calls=%fused_computation.2 | convolution fusion | flops 319504000 | bytes 4917248 | tf_op jit(solution)/shard_map/ij,bjd->bid/dot_general | solution.py:568
  10.0 0.0 copy-start.14
  10.1 0.0 copy-done.16
  10.1 0.9 multiply_convert_fusion
  11.0 0.0 copy-done
  11.0 0.0 copy-start.23
  11.0 2.3 %convolution_convert_fusion.1.v_ref = bf16[384,512]{1,0:T(8,128)(2,1)} fusion(bf16[384,3200]{1,0:T(8,128)(2,1)S(1)} %multiply_convert_fusion, bf16[3200,512]{1,0:T(8,128)(2,1)S(1)} %copy-done), kind=kOutput, calls=%fused_computation.5 | convolution fusion | flops 1258487808 | bytes 6127616 | tf_op jit(solution)/shard_map/dot_general | solution.py:580
  13.2 0.0 copy-done.14
  13.3 0.0 copy-done.23
  13.3 0.0 copy-start.24
  13.3 2.2 %convolution_convert_fusion.2.k_ref = bf16[384,512]{1,0:T(8,128)(2,1)} fusion(bf16[384,3200]{1,0:T(8,128)(2,1)S(1)} %multiply_convert_fusion, bf16[3200,512]{1,0:T(8,128)(2,1)S(1)} %copy-done.23), kind=kOutput, calls=%fused_computation.6 | convolution fusion | flops 1258487808 | bytes 6127616 | tf_op jit(solution)/shard_map/dot_general | solution.py:579
  15.5 0.0 copy-done.24
  15.5 2.3 %fusion.q_ref = bf16[384,512]{1,0:T(8,128)(2,1)} fusion(bf16[384,3200]{1,0:T(8,128)(2,1)S(1)} %multiply_convert_fusion, bf16[3200,512]{1,0:T(8,128)(2,1)S(1)} %copy-done.24), kind=kOutput, calls=%fused_computation.4 | convolution fusion | flops 1258684416 | bytes 6127616 | tf_op jit(solution)/shard_map/dot_general | solution.py:577
  17.7 0.0 copy-start.25
  17.8 0.0 copy-start.20
  17.8 0.0 copy-start.21
  17.8 1.3 dynamic-slice_bitcast_fusion.3
  19.1 0.1 pad_maximum_fusion.w_ref
  19.2 0.0 copy-start.11
  19.2 1.0 copy-done.11
  20.2 1.0 copy-done.12
  21.2 1.0 copy-done.13
  22.2 22.4 %exchange_heads.1 = (bf16[8,384,128]{2,1,0:T(8,128)(2,1)S(1)}, bf16[8,384,128]{2,1,0:T(8,128)(2,1)S(1)}, bf16[8,384,128]{2,1,0:T(8,128)(2,1)}, bf16[4,64,800]{2,1,0:T(8,128)(2,1)S(1)}) custom-call(bf16[384,512]{1,0:T(8,128)(2,1)S(1)} %copy-done.13, bf16[384,512]{1,0:T(8,128)(2,1)S(1)} %copy-done.12, bf16[384,512]{1,0:T(8,128)(2,1)S(1)} %copy-done.11, ...), custom_call_target="tpu_custom_call" | custom-call | tf_op jit(solution)/shard_map/exchange_heads/pallas_call | solution.py:118
  44.6 0.0 copy-start.5
  44.7 0.9 copy-done.5
  45.6 0.9 copy-done.7
  46.4 0.8 copy-done.10
  47.3 0.0 all-gather.3.cloned.1.call-update
  47.3 0.0 copy-done.25
  47.3 0.2 reduce-window.8
  47.5 0.1 fusion.7
  47.6 0.1 compare_select_fusion
  47.6 0.1 select_n.85
  47.7 0.8 dynamic_slice.11
  48.5 0.0 copy-done.17
  48.5 0.0 copy-done.18
  48.5 0.0 copy-done.19
  48.6 0.0 copy-done.20
  48.6 0.0 copy-done.21
  48.6 0.1 broadcast_in_dim.22.bias_ref
  48.7 1.1 copy-done.6
  49.8 1.1 copy-done.8
  51.0 1.1 copy-done.9
  52.1 41.0 %attend_and_spread.1.a_ref = bf16[384,2048]{1,0:T(8,128)(2,1)S(1)} custom-call(bf16[8,384,128]{2,1,0:T(8,128)(2,1)S(1)} %copy-done.6, bf16[3072,128]{1,0:T(8,128)(2,1)S(1)} %bitcast.35, bf16[3072,128]{1,0:T(8,128)(2,1)S(1)} %bitcast.36, f32[9,1,128]{2,1,0:T(1,128)S(1)} %broadcast_in_dim.22.bias_ref), custom_call_target="tpu_custom_call" | custom-call | tf_op jit(solution)/shard_map/attend_and_spread/pallas_call | solution.py:209
  93.1 0.0 copy-start.1
  93.1 1.2 copy-done.1
  94.3 0.0 copy-done.22
  94.3 0.2 compare_reduce_fusion
  94.4 2.3 %constant_dynamic-slice_fusion.x_ref = bf16[384,800]{1,0:T(8,128)(2,1)} fusion(bf16[384,3200]{1,0:T(8,128)(2,1)} %bitcast.38, s32[]{:T(128)S(6)} %select_n.86), kind=kLoop, calls=%fused_computation.47 | loop fusion | bytes 1228804 | tf_op jit(solution)/shard_map/dynamic_slice | solution.py:594
  96.8 0.0 copy-done.15
  96.8 1.0 convolution_convert_fusion.3.text_ref
  97.9 0.0 all-gather.3.cloned.1.call-done
  97.9 0.0 copy-start.2
  97.9 1.4 copy-done.2
  99.3 1.1 copy-done.3
  100.4 47.7 %merge_rows.1 = bf16[8,96,3200]{2,1,0:T(8,128)(2,1)} custom-call(bf16[384,2048]{1,0:T(8,128)(2,1)S(1)} %copy-done.2, bf16[8,4,64,800]{3,2,1,0:T(8,128)(2,1)} %bitcast.39, bf16[384,800]{1,0:T(8,128)(2,1)S(1)} %copy-done.3, f32[1,800]{1,0:T(1,128)S(1)} %reshape.189.ls_ref, f32[8,3584]{1,0:T(8,128)S(1)} %select_maximum_fusion.affine_ref), custom_call_target="tpu_custom_call" | custom-call | tf_op jit(solution)/shard_map/merge_rows/pallas_call | solution.py:346
  148.1 0.1 broadcast_in_dim.42.mask_ref
  148.2 0.0 copy-done.4
  148.2 66.2 %finish_rows.1 = (bf16[112,1536]{1,0:T(8,128)(2,1)S(1)}, bf16[112,1536]{1,0:T(8,128)(2,1)S(1)}) custom-call(bf16[768,3200]{1,0:T(8,128)(2,1)} %bitcast.37, bf16[3200,768]{1,0:T(8,128)(2,1)} %w_ref.1, s32[1,768]{1,0:T(1,128)S(1)} %reshape.191.slot_ref, f32[1,768]{1,0:T(1,128)S(1)} %reshape.192.bias_ref, bf16[224,768]{1,0:T(8,128)(2,1)S(1)} %copy-done.4, ...), custom_call_target="tpu_custom_call" | custom-call | tf_op jit(solution)/shard_map/finish_rows/pallas_call | solution.py:503
  214.4 0.7 copy.20
  215.1 0.7 copy.21
  (25 shorter events, 0.1 us)
Async XLA Ops:
  7.2 3.8 %copy-start = (bf16[3200,512]{1,0:T(8,128)(2,1)S(1)}, bf16[3200,512]{1,0:T(8,128)(2,1)}, u32[]{:S(2)}) copy-start(bf16[3200,512]{1,0:T(8,128)(2,1)} %param.20) | copy-start | bytes 9830404
  7.2 2.9 %copy-start.16 = (f32[3200]{0:T(1024)S(1)}, f32[3200]{0:T(1024)}, u32[]{:S(2)}) copy-start(f32[3200]{0:T(1024)} %param.17) | copy-start | bytes 38404
  7.2 90.7 %all-gather.3.cloned.1.call-start = ((), (), s32[]{:S(2)}) async-start(), calls=%async_computation | async-start | bytes 4128768 | tf_op jit(solution)/shard_map/all_gather | solution.py:585
  10.0 3.2 %copy-start.14 = (bf16[128,3,3200]{2,0,1:T(8,128)(2,1)}, bf16[128,3,3200]{2,0,1:T(8,128)(2,1)S(1)}, u32[]{:S(2)}) copy-start(bf16[128,3,3200]{2,0,1:T(8,128)(2,1)S(1)} %get-tuple-element.15) | copy-start | bytes 7372804
  11.0 2.3 %copy-start.23 = (bf16[3200,512]{1,0:T(8,128)(2,1)S(1)}, bf16[3200,512]{1,0:T(8,128)(2,1)}, u32[]{:S(2)}) copy-start(bf16[3200,512]{1,0:T(8,128)(2,1)} %param.19) | copy-start | bytes 9830404
  13.3 2.2 %copy-start.24 = (bf16[3200,512]{1,0:T(8,128)(2,1)S(1)}, bf16[3200,512]{1,0:T(8,128)(2,1)}, u32[]{:S(2)}) copy-start(bf16[3200,512]{1,0:T(8,128)(2,1)} %param.18) | copy-start | bytes 9830404
  17.7 29.5 %copy-start.25 = (s32[2]{0:T(128)S(1)}, s32[2]{0:T(128)}, u32[]{:S(2)}) copy-start(s32[2]{0:T(128)} %param.29) | copy-start | bytes 28
  17.8 30.8 %copy-start.17 = (f32[3200]{0:T(1024)S(1)}, f32[3200]{0:T(1024)}, u32[]{:S(2)}) copy-start(f32[3200]{0:T(1024)} %param.23) | copy-start | bytes 38404
  17.8 30.8 %copy-start.18 = (f32[3200]{0:T(1024)S(1)}, f32[3200]{0:T(1024)}, u32[]{:S(2)}) copy-start(f32[3200]{0:T(1024)} %param.24) | copy-start | bytes 38404
  17.8 30.8 %copy-start.19 = (f32[1536]{0:T(1024)S(1)}, f32[1536]{0:T(1024)}, u32[]{:S(2)}) copy-start(f32[1536]{0:T(1024)} %param.28) | copy-start | bytes 18436
  17.8 30.8 %copy-start.20 = (s32[768]{0:T(1024)S(1)}, s32[768]{0:T(1024)}, u32[]{:S(2)}) copy-start(s32[768]{0:T(1024)} %param.30) | copy-start | bytes 9220
  17.8 30.8 %copy-start.21 = (f32[768]{0:T(1024)S(1)}, f32[768]{0:T(1024)}, u32[]{:S(2)}) copy-start(f32[768]{0:T(1024)} %param.26) | copy-start | bytes 9220
  19.2 1.0 copy-start.11
  20.2 1.0 copy-start.12
  21.2 1.0 copy-start.13
  22.2 72.1 %copy-start.22 = (s32[128]{0:T(128)S(1)}, s32[128]{0:T(128)}, u32[]{:S(2)}) copy-start(s32[128]{0:T(128)} %param.31) | copy-start | bytes 1540
  44.6 0.9 copy-start.5
  45.6 0.9 copy-start.7
  46.4 0.8 copy-start.10
  47.3 49.5 %copy-start.15 = (bf16[128,768]{1,0:T(8,128)(2,1)S(1)}, bf16[128,768]{1,0:T(8,128)(2,1)}, u32[]{:S(2)}) copy-start(bf16[128,768]{1,0:T(8,128)(2,1)} %param.27) | copy-start | bytes 589828
  48.7 1.1 copy-start.6
  49.8 1.1 copy-start.8
  51.0 1.1 copy-start.9
  93.1 1.2 copy-start.1
  97.9 1.4 copy-start.2
  99.3 1.1 copy-start.3
  100.4 47.8 %copy-start.4 = (bf16[224,768]{1,0:T(8,128)(2,1)S(1)}, bf16[224,768]{1,0:T(8,128)(2,1)}, u32[]{:S(2)}) copy-start(bf16[224,768]{1,0:T(8,128)(2,1)} %convolution_convert_fusion.3.text_ref) | copy-start | bytes 1032196
Sparse Core Ops, SparseCore 0:
  47.4 49.4 all-gather.2
